TPU v7x, 256 devices: a whole 4x4x8 slice. The times are simulated.
256 devices in a mesh: group: 16 (over x, z_lo, core), seq: 16 (over y, z_hi).
Axes of the slice: x: 4, y: 4, z: 8 (z_hi: 4, z_lo: 2; z = z_hi * 2 + z_lo), core: 2. Of those that a mesh axis runs over, the one named last changes fastest.
Arguments:
- step_inputs: bfloat16 [4, 64, 8192], P(None, 'group', 'seq'), may hold values from -6 to 6
- norm_gain: bfloat16 [8192], P('seq'), may hold values from 0.5 to 2
- w_query: bfloat16 [8192, 4096], P('seq'), may hold values from -0.0625 to 0.0625
- w_keyval: bfloat16 [8192, 1024], P('seq'), may hold values from -0.0625 to 0.0625
- w_out: bfloat16 [4096, 8192], P('seq'), may hold values from -0.25 to 0.25
- key_cache: bfloat16 [64, 512, 512], P('group', 'seq'), may hold values from -420 to 420
- value_cache: bfloat16 [64, 512, 512], P('group', 'seq'), may hold values from -6 to 6
- ctx_len: int32 [64], P('group'), may hold values from 2 to 512, as said below
- mig_slot: int32 [4, 16], replicated, may hold values from 0 to 3
- mig_shift: int32 [4], replicated, may hold values from 1 to 15, as said below
Outputs:
- attn_output: bfloat16 [4, 64, 8192], P(None, 'group', 'seq')
Inputs may be any that keep to these rules, and one draw needn't show every extreme that they name: `ctx_len`: at least two cached positions per slot; some slot holds all 512. Group g sends to group (g + mig_shift[s]) mod 16.
All inputs are finite; a program needn't handle non-finite values.
Results may differ from a plain program's by a relative error of at most 0.034.
Values may be sent and summed in bfloat16 or wider, within the bound.
No kernel may reach another device: no remote copies, remote signals or barrier semaphores. Data moves between devices by JAX's collectives and lax.ppermute only.
A program may use at most 128 MiB of HBM per device.

v0:
```python
import jax
import jax.numpy as jnp
from jax import lax
from jax.sharding import PartitionSpec as P

D = 8192
H = 32
KVH = 4
HD = 128
STEPS = 4


norm_eps = 1e-06
rope_base = 1000000.0
masked_score = -1e30


def merged(array, axis, combine):
    everything = jax.tree.map(
        lambda part, kind: lax.all_gather(part.astype(kind), axis),
        array,
        (jnp.bfloat16, jnp.bfloat16, jnp.bfloat16),
    )

    def take(k):
        return jax.tree.map(lambda part, own: part[k].astype(own.dtype), everything, array)

    return lax.fori_loop(
        1, lax.axis_size(axis), lambda k, so_far: combine(so_far, take(k)), take(0)
    )


def rotary(values, position):
    half = values.shape[-1] // 2
    exponent = jnp.arange(half, dtype=jnp.float32) * (2.0 / values.shape[-1])
    inverse = jnp.power(jnp.float32(rope_base), -exponent)
    angles = position.astype(jnp.float32)[..., None, None] * inverse
    cosine = jnp.cos(angles)
    sine = jnp.sin(angles)
    first = values[..., :half]
    second = values[..., half:]
    return jnp.concatenate(
        [first * cosine - second * sine, second * cosine + first * sine], axis=-1
    )


def merge_parts(first, second):
    peak_a, total_a, summed_a = first
    peak_b, total_b, summed_b = second
    top = jnp.maximum(peak_a, peak_b)
    factor_a = jnp.exp(peak_a - top)
    factor_b = jnp.exp(peak_b - top)
    return (
        top,
        total_a * factor_a + total_b * factor_b,
        summed_a * factor_a[..., None] + summed_b * factor_b[..., None],
    )


def partial_softmax(queries, keys, values, live):
    scale = 1.0 / jnp.sqrt(jnp.float32(HD))
    scores = (
        jnp.einsum("rkgd,rckd->rkgc", queries, keys, preferred_element_type=jnp.float32) * scale
    )
    peak = jnp.max(jnp.where(live, scores, masked_score), axis=-1)
    weights = jnp.where(live, jnp.exp(scores - peak[..., None]), 0.0)
    total = jnp.sum(weights, axis=-1)
    summed = jnp.einsum(
        "rkgc,rckd->rkgd", weights.astype(jnp.bfloat16), values, preferred_element_type=jnp.float32
    )
    requests = queries.shape[0]
    return (peak.reshape(requests, H), total.reshape(requests, H), summed.reshape(requests, H, HD))


def body(
    step_inputs,
    norm_gain,
    w_query,
    w_keyval,
    w_out,
    key_cache,
    value_cache,
    ctx_len,
    mig_slot,
    mig_shift,
):
    requests = key_cache.shape[0]
    local_ctx = key_cache.shape[1]
    kv_width = key_cache.shape[2]
    per_kv = H // KVH
    seq_count = lax.axis_size("seq")
    group_count = lax.axis_size("group")
    own_heads = H // seq_count
    group_index = lax.axis_index("group")
    seq_index = lax.axis_index("seq")
    head_start = seq_index * own_heads
    all_lengths = lax.all_gather(ctx_len, "group", axis=0, tiled=True).reshape(
        group_count, requests
    )
    recent_keys = jnp.zeros((requests, STEPS, kv_width), jnp.bfloat16)
    recent_values = jnp.zeros((requests, STEPS, kv_width), jnp.bfloat16)
    offsets = seq_index * local_ctx + jnp.arange(local_ctx, dtype=jnp.int32)
    group_ids = jnp.arange(group_count, dtype=jnp.int32)
    slot_ids = jnp.arange(requests, dtype=jnp.int32)
    gain_f = norm_gain.astype(jnp.float32)
    results = []
    for step in range(STEPS):
        shift = mig_shift[step]
        slots = mig_slot[step]
        source = (group_index - shift) % group_count
        out_slot = lax.dynamic_index_in_dim(slots, group_index, 0, keepdims=False)
        send_keys = lax.dynamic_index_in_dim(key_cache, out_slot, 0, keepdims=True)
        send_values = lax.dynamic_index_in_dim(value_cache, out_slot, 0, keepdims=True)
        send_recent_keys = lax.dynamic_index_in_dim(recent_keys, out_slot, 0, keepdims=True)
        send_recent_values = lax.dynamic_index_in_dim(recent_values, out_slot, 0, keepdims=True)

        def pick_source(carry, pieces, start, source=source):
            count = pieces[0].shape[0]
            inside = jnp.logical_and(source >= 0, source < count)
            chosen = jnp.clip(source, 0, count - 1)
            return tuple(
                (
                    jnp.where(
                        inside, lax.dynamic_index_in_dim(piece, chosen, 0, keepdims=True), held
                    )
                    for piece, held in zip(pieces, carry)
                )
            )

        start_carry = (
            jnp.zeros_like(send_keys),
            jnp.zeros_like(send_values),
            jnp.zeros_like(send_recent_keys),
            jnp.zeros_like(send_recent_values),
        )
        got_keys, got_values, got_recent_keys, got_recent_values = pick_source(
            start_carry,
            (
                lax.all_gather(send_keys, "group", axis=0, tiled=True),
                lax.all_gather(send_values, "group", axis=0, tiled=True),
                lax.all_gather(send_recent_keys, "group", axis=0, tiled=True),
                lax.all_gather(send_recent_values, "group", axis=0, tiled=True),
            ),
            jnp.int32(0),
        )
        key_cache = lax.dynamic_update_slice_in_dim(key_cache, got_keys, out_slot, 0)
        value_cache = lax.dynamic_update_slice_in_dim(value_cache, got_values, out_slot, 0)
        recent_keys = lax.dynamic_update_slice_in_dim(recent_keys, got_recent_keys, out_slot, 0)
        recent_values = lax.dynamic_update_slice_in_dim(
            recent_values, got_recent_values, out_slot, 0
        )
        source_all = (group_ids - shift) % group_count
        moved_lengths = all_lengths[source_all, slots[source_all]]
        all_lengths = jnp.where(
            slot_ids[None, :] == slots[:, None], moved_lengths[:, None], all_lengths
        )
        lengths = lax.dynamic_index_in_dim(all_lengths, group_index, 0, keepdims=False)
        inputs = step_inputs[step].astype(jnp.float32)
        square_part = jnp.sum(inputs * inputs, axis=-1)
        normed = (inputs * gain_f).astype(jnp.bfloat16)
        query_part = jnp.dot(normed, w_query, preferred_element_type=jnp.float32)
        keyval_part = jnp.dot(normed, w_keyval, preferred_element_type=jnp.float32)
        squares, query_full, keyval_full = lax.psum((square_part, query_part, keyval_part), "seq")
        inverse = lax.rsqrt(squares / D + norm_eps)[:, None]
        position = lengths + step
        queries = rotary((query_full * inverse).reshape(requests, H, HD), position).astype(
            jnp.bfloat16
        )
        keyval_full = keyval_full * inverse
        new_key = (
            rotary(keyval_full[:, :kv_width].reshape(requests, KVH, HD), position)
            .reshape(requests, kv_width)
            .astype(jnp.bfloat16)
        )
        new_value = keyval_full[:, kv_width:].astype(jnp.bfloat16)
        recent_keys = recent_keys.at[:, step].set(new_key)
        recent_values = recent_values.at[:, step].set(new_value)
        grouped = queries.reshape(requests, KVH, per_kv, HD)
        live = (offsets[None, :] < lengths[:, None])[:, None, None, :]
        peak, total, summed = partial_softmax(
            grouped,
            key_cache.reshape(requests, local_ctx, KVH, HD),
            value_cache.reshape(requests, local_ctx, KVH, HD),
            live,
        )
        recent_live = (jnp.arange(STEPS, dtype=jnp.int32) <= step)[None, None, None, :]
        recent_peak, recent_total, recent_summed = partial_softmax(
            grouped,
            recent_keys.reshape(requests, STEPS, KVH, HD),
            recent_values.reshape(requests, STEPS, KVH, HD),
            recent_live,
        )
        recent_peak = lax.dynamic_slice_in_dim(recent_peak, head_start, own_heads, 1)
        recent_total = lax.dynamic_slice_in_dim(recent_total, head_start, own_heads, 1)
        recent_summed = lax.dynamic_slice_in_dim(recent_summed, head_start, own_heads, 1)
        peak_all, total_all, summed_all = merged((peak, total, summed), "seq", merge_parts)
        peak_own = lax.dynamic_slice_in_dim(peak_all, head_start, own_heads, 1)
        total_own = lax.dynamic_slice_in_dim(total_all, head_start, own_heads, 1)
        summed_own = lax.dynamic_slice_in_dim(summed_all, head_start, own_heads, 1)
        top = jnp.maximum(peak_own, recent_peak)
        cache_factor = jnp.exp(peak_own - top)
        recent_factor = jnp.exp(recent_peak - top)
        combined_total = total_own * cache_factor + recent_total * recent_factor
        combined = summed_own * cache_factor[..., None] + recent_summed * recent_factor[..., None]
        attention = (
            (combined / combined_total[..., None])
            .reshape(requests, own_heads * HD)
            .astype(jnp.bfloat16)
        )
        projected = jnp.dot(attention, w_out, preferred_element_type=jnp.float32)
        reduced = lax.psum_scatter(
            projected.astype(jnp.bfloat16), "seq", scatter_dimension=1, tiled=True
        )
        results.append(reduced)
    return jnp.stack(results)


def solution(mesh):
    placed = (
        P(None, "group", "seq"),
        P("seq"),
        P("seq", None),
        P("seq", None),
        P("seq", None),
        P("group", "seq", None),
        P("group", "seq", None),
        P("group"),
        P(),
        P(),
    )
    return jax.shard_map(
        body, mesh=mesh, in_specs=placed, out_specs=P(None, "group", "seq"), check_vma=False
    )
```

profile of v0, /device:TPU:32, one launch (start us, length us, event | category | flops | bytes accessed | tf_op | source)
XLA Modules:
  0.0 1360.6 jit_solution(13749046825283366993)
XLA Ops:
  60.2 19.0 %all_gather.99 = bf16[16,32,512]{2,1,0:T(8,128)(2,1)S(1)} all-gather(bf16[1,32,512]{2,1,0:T(8,128)(2,1)S(1)} %constant_dynamic-slice_fusion.50), channel_id=1, replica_groups=mesh['group'=16,'seq'=16] {'group'}, dimensions={0}, use_global_device_ids=true | all-gather | bytes 557056 | tf_op jit(solution)/shard_map/all_gather | solution.py:140
  79.9 20.3 %all_gather.104 = bf16[16,32,512]{2,1,0:T(8,128)(2,1)S(1)} all-gather(bf16[1,32,512]{2,1,0:T(8,128)(2,1)S(1)} %constant_dynamic-slice_fusion.38), channel_id=1, replica_groups=mesh['group'=16,'seq'=16] {'group'}, dimensions={0}, use_global_device_ids=true | all-gather | bytes 557056 | tf_op jit(solution)/shard_map/all_gather | solution.py:140
  118.6 21.5 %all_gather.101 = bf16[16,32,512]{2,1,0:T(8,128)(2,1)S(1)} all-gather(bf16[1,32,512]{2,1,0:T(8,128)(2,1)S(1)} %constant_dynamic-slice_fusion.40), channel_id=1, replica_groups=mesh['group'=16,'seq'=16] {'group'}, dimensions={0}, use_global_device_ids=true | all-gather | bytes 557056 | tf_op jit(solution)/shard_map/all_gather | solution.py:139
  142.8 30.6 %all-reduce.6.cloned.1.call-done = (f32[4,1024]{1,0:T(4,128)}, f32[4]{0:T(128)}, f32[4,1024]{1,0:T(4,128)}, f32[4]{0:T(128)}, f32[4,1024]{1,0:T(4,128)}, /*index=5*/f32[4]{0:T(128)}, f32[4,1024]{1,0:T(4,128)}, f32[4]{0:T(128)}) async-done(((f32[4,1024]{1,0:T(4,128)}, f32[4]{0:T(128)}, f32[4,1024]{1,0:T(4,128)}, f32[4]{0:T(128)}, f32[4,1024]{1,0:T(4,128)}, /*index=5*/f32[4]{0:T(128)}, f32[4,1024]{1,0:T(4,128)}, ...) | async-done | bytes 65616 | tf_op jit(solution)/shard_map/psum | solution.py:163
  196.1 19.0 %all_gather.107 = bf16[16,4,512]{2,1,0:T(4,128)(2,1)S(1)} all-gather(bf16[1,4,512]{2,1,0:T(4,128)(2,1)S(1)} %constant_dynamic-slice_fusion.32), channel_id=1, replica_groups=mesh['group'=16,'seq'=16] {'group'}, dimensions={0}, use_global_device_ids=true | all-gather | bytes 69632 | tf_op jit(solution)/shard_map/all_gather | solution.py:142
  215.1 124.0 %all-reduce.8.cloned.1.call-done = (f32[4,4096]{1,0:T(4,128)}, f32[4,4096]{1,0:T(4,128)}, f32[4,4096]{1,0:T(4,128)}, f32[4,4096]{1,0:T(4,128)}) async-done(((f32[4,4096]{1,0:T(4,128)}, f32[4,4096]{1,0:T(4,128)}, f32[4,4096]{1,0:T(4,128)}, f32[4,4096]{1,0:T(4,128)}), (f32[4,4096]{1,0:T(4,128)}, f32[4,4096]{1,0:T(4,128)}, f32[4,4096]{1,0:T(4,128)}, f32[4,4096]{1,0:T(4,128)})) %all-reduce.8.cloned.1.call-update) | async-done | bytes 262160 | tf_op jit(solution)/shard_map/psum | solution.py:163
  380.7 45.7 %all_gather.100 = bf16[16,4,32,128]{3,2,1,0:T(8,128)(2,1)S(1)} all-gather(bf16[1,4,32,128]{3,2,1,0:T(8,128)(2,1)S(1)} %fusion.12), channel_id=1, replica_groups=mesh['group'=16,'seq'=16] {'seq'}, dimensions={0}, use_global_device_ids=true | all-gather | bytes 557056 | tf_op jit(solution)/shard_map/all_gather | solution.py:20
  427.3 42.5 %all_gather.105 = bf16[16,4,32,128]{3,2,1,0:T(8,128)(2,1)S(1)} all-gather(bf16[1,4,32,128]{3,2,1,0:T(8,128)(2,1)S(1)} %fusion.13), channel_id=1, replica_groups=mesh['group'=16,'seq'=16] {'seq'}, dimensions={0}, use_global_device_ids=true | all-gather | bytes 557056 | tf_op jit(solution)/shard_map/all_gather | solution.py:20
  487.2 21.4 %all_gather.111 = bf16[16,32,512]{2,1,0:T(8,128)(2,1)S(1)} all-gather(bf16[1,32,512]{2,1,0:T(8,128)(2,1)S(1)} %constant_dynamic-slice_fusion.24), channel_id=1, replica_groups=mesh['group'=16,'seq'=16] {'group'}, dimensions={0}, use_global_device_ids=true | all-gather | bytes 557056 | tf_op jit(solution)/shard_map/all_gather | solution.py:140
  545.0 39.8 %all_gather.98 = bf16[16,4,32]{2,1,0:T(4,128)(2,1)S(1)} all-gather(bf16[1,4,32]{2,1,0:T(4,128)(2,1)S(1)} %convert_element_type.573), channel_id=1, replica_groups=mesh['group'=16,'seq'=16] {'seq'}, dimensions={0}, use_global_device_ids=true | all-gather | bytes 4352 | tf_op jit(solution)/shard_map/all_gather | solution.py:20
  584.8 39.1 %all_gather.97 = bf16[16,4,32]{2,1,0:T(4,128)(2,1)S(1)} all-gather(bf16[1,4,32]{2,1,0:T(4,128)(2,1)S(1)} %convert_element_type.569), channel_id=1, replica_groups=mesh['group'=16,'seq'=16] {'seq'}, dimensions={0}, use_global_device_ids=true | all-gather | bytes 4352 | tf_op jit(solution)/shard_map/all_gather | solution.py:20
  626.6 39.7 %all_gather.103 = bf16[16,4,32]{2,1,0:T(4,128)(2,1)S(1)} all-gather(bf16[1,4,32]{2,1,0:T(4,128)(2,1)S(1)} %convert_element_type.595), channel_id=1, replica_groups=mesh['group'=16,'seq'=16] {'seq'}, dimensions={0}, use_global_device_ids=true | all-gather | bytes 4352 | tf_op jit(solution)/shard_map/all_gather | solution.py:20
  666.3 39.1 %all_gather.102 = bf16[16,4,32]{2,1,0:T(4,128)(2,1)S(1)} all-gather(bf16[1,4,32]{2,1,0:T(4,128)(2,1)S(1)} %convert_element_type.591), channel_id=1, replica_groups=mesh['group'=16,'seq'=16] {'seq'}, dimensions={0}, use_global_device_ids=true | all-gather | bytes 4352 | tf_op jit(solution)/shard_map/all_gather | solution.py:20
  708.1 39.7 %all_gather.109 = bf16[16,4,32]{2,1,0:T(4,128)(2,1)S(1)} all-gather(bf16[1,4,32]{2,1,0:T(4,128)(2,1)S(1)} %convert_element_type.613), channel_id=1, replica_groups=mesh['group'=16,'seq'=16] {'seq'}, dimensions={0}, use_global_device_ids=true | all-gather | bytes 4352 | tf_op jit(solution)/shard_map/all_gather | solution.py:20
  747.9 39.1 %all_gather.110 = bf16[16,4,32]{2,1,0:T(4,128)(2,1)S(1)} all-gather(bf16[1,4,32]{2,1,0:T(4,128)(2,1)S(1)} %convert_element_type.617), channel_id=1, replica_groups=mesh['group'=16,'seq'=16] {'seq'}, dimensions={0}, use_global_device_ids=true | all-gather | bytes 4352 | tf_op jit(solution)/shard_map/all_gather | solution.py:20
  806.1 39.8 %all_gather.116 = bf16[16,4,32]{2,1,0:T(4,128)(2,1)S(1)} all-gather(bf16[1,4,32]{2,1,0:T(4,128)(2,1)S(1)} %convert_element_type.635), channel_id=1, replica_groups=mesh['group'=16,'seq'=16] {'seq'}, dimensions={0}, use_global_device_ids=true | all-gather | bytes 4352 | tf_op jit(solution)/shard_map/all_gather | solution.py:20
  845.9 39.1 %all_gather.117 = bf16[16,4,32]{2,1,0:T(4,128)(2,1)S(1)} all-gather(bf16[1,4,32]{2,1,0:T(4,128)(2,1)S(1)} %convert_element_type.639), channel_id=1, replica_groups=mesh['group'=16,'seq'=16] {'seq'}, dimensions={0}, use_global_device_ids=true | all-gather | bytes 4352 | tf_op jit(solution)/shard_map/all_gather | solution.py:20
  885.0 43.0 %all_gather.112 = bf16[16,4,32,128]{3,2,1,0:T(8,128)(2,1)S(1)} all-gather(bf16[1,4,32,128]{3,2,1,0:T(8,128)(2,1)S(1)} %fusion.14), channel_id=1, replica_groups=mesh['group'=16,'seq'=16] {'seq'}, dimensions={0}, use_global_device_ids=true | all-gather | bytes 557056 | tf_op jit(solution)/shard_map/all_gather | solution.py:20
  930.5 20.3 %all_gather.118 = bf16[16,32,512]{2,1,0:T(8,128)(2,1)S(1)} all-gather(bf16[1,32,512]{2,1,0:T(8,128)(2,1)S(1)} %constant_dynamic-slice_fusion.9), channel_id=1, replica_groups=mesh['group'=16,'seq'=16] {'group'}, dimensions={0}, use_global_device_ids=true | all-gather | bytes 557056 | tf_op jit(solution)/shard_map/all_gather | solution.py:140
  951.0 41.6 %all_gather.119 = bf16[16,4,32,128]{3,2,1,0:T(8,128)(2,1)S(1)} all-gather(bf16[1,4,32,128]{3,2,1,0:T(8,128)(2,1)S(1)} %fusion.15), channel_id=1, replica_groups=mesh['group'=16,'seq'=16] {'seq'}, dimensions={0}, use_global_device_ids=true | all-gather | bytes 557056 | tf_op jit(solution)/shard_map/all_gather | solution.py:20
  1015.4 67.7 %reduce-scatter.19.cloned.1.call-done = bf16[512,4]{1,0:T(8,128)(2,1)} async-done(((bf16[8192,4]{1,0:T(8,128)(2,1)}), bf16[512,4]{1,0:T(8,128)(2,1)}) %reduce-scatter.19.cloned.1.call-update) | async-done | bytes 4112
  1084.1 88.8 %reduce-scatter.17.cloned.1.call-done = bf16[512,4]{1,0:T(8,128)(2,1)} async-done(((bf16[8192,4]{1,0:T(8,128)(2,1)}), bf16[512,4]{1,0:T(8,128)(2,1)}) %reduce-scatter.17.cloned.1.call-update) | async-done | bytes 4112
  1173.9 88.4 %reduce-scatter.15.cloned.1.call-done = bf16[512,4]{1,0:T(8,128)(2,1)} async-done(((bf16[8192,4]{1,0:T(8,128)(2,1)}), bf16[512,4]{1,0:T(8,128)(2,1)}) %reduce-scatter.15.cloned.1.call-update) | async-done | bytes 4112
  1263.2 88.8 %reduce-scatter.13.cloned.1.call-done = bf16[512,4]{1,0:T(8,128)(2,1)} async-done(((bf16[8192,4]{1,0:T(8,128)(2,1)}), bf16[512,4]{1,0:T(8,128)(2,1)}) %reduce-scatter.13.cloned.1.call-update) | async-done | bytes 4112
  (373 shorter events, 245.9 us)
Async XLA Ops:
  6.5 4.1 copy-start
  6.5 10.3 copy-start.2
  6.5 166.9 %all-reduce.6.cloned.1.call-start = ((), (), s32[]{:S(2)}) async-start(), calls=%async_computation.8 | async-start | bytes 135168 | tf_op jit(solution)/shard_map/psum | solution.py:163
  16.8 322.4 %all-reduce.8.cloned.1.call-start = ((), (), s32[]{:S(2)}) async-start(), calls=%async_computation.9 | async-start | bytes 524288 | tf_op jit(solution)/shard_map/psum | solution.py:163
  16.8 3.6 copy-start.1
  21.7 2.7 copy-start.3
  21.7 8.1 copy-start.4
  21.7 14.3 %copy-start.6 = (u32[256]{0:T(256)S(1)}, u32[256]{0:T(256)}, u32[]{:S(2)}) copy-start(u32[256]{0:T(256)} %constant.582) | copy-start | bytes 3076
  21.7 15.6 %copy-start.5 = (s32[4]{0:T(128)S(1)}, s32[4]{0:T(128)}, u32[]{:S(2)}) copy-start(s32[4]{0:T(128)} %param.41) | copy-start | bytes 52
  24.3 1058.8 %reduce-scatter.19.cloned.1.call-start = ((), (), s32[]{:S(2)}) async-start(), calls=%async_computation.7 | async-start | bytes 2228224
  1000.0 172.9 %reduce-scatter.17.cloned.1.call-start = ((), (), s32[]{:S(2)}) async-start(), calls=%async_computation.6 | async-start | bytes 2228224
  1005.3 257.0 %reduce-scatter.15.cloned.1.call-start = ((), (), s32[]{:S(2)}) async-start(), calls=%async_computation.5 | async-start | bytes 2228224
  1010.5 341.6 %reduce-scatter.13.cloned.1.call-start = ((), (), s32[]{:S(2)}) async-start(), calls=%async_computation.4 | async-start | bytes 2228224
Sparse Core Ops, SparseCore 0:
  16.9 156.4 all-reduce.5
  176.5 162.6 all-reduce.7
  1000.2 82.9 reduce-scatter.18
  1087.0 85.8 reduce-scatter.16
  1176.3 85.8 reduce-scatter.14
  1266.1 85.9 reduce-scatter.12
where the time goes:
time: 1360 us
  blocking collectives  764 us (56%)
  waiting for transfers between devices  488 us (36%)
  matrix products  29.1 us (2%)
  other arithmetic  27.5 us (2%)
  local copies, waits for them, and re-layouts  25 us (2%)
  between operations  24.9 us (2%)
    all_gather x12, blocking collectives, merged(): lax.all_gather(part.astype(kind), axis)  488 us
    unnamed x10, waiting for transfers between devices  334 us
    psum x2, waiting for transfers between devices, body(): lax.psum((square_part, query_part, keyval_part), 'seq')  155 us
    all_gather x4, blocking collectives, body(): lax.all_gather(send_values, 'group', axis=0, tiled=True)  81.1 us
    all_gather x4, blocking collectives, body(): lax.all_gather(send_keys, 'group', axis=0, tiled=True)  75.1 us
    all_gather x3, blocking collectives, body(): lax.all_gather(send_recent_keys, 'group', axis=0, tiled=True)  54.5 us
    all_gather x3, blocking collectives, body(): lax.all_gather(send_recent_values, 'group', axis=0, tiled=True)  53.2 us
  transfers between devices with their start and end apart: 6, of which 6 were waited for; matrix products, arithmetic and copies ran while one was open for 3% of the time, Pallas kernels for 0%

commit v1 on v0

v1 whole, which is shorter than its diff:
```python
import functools

import jax
import jax.numpy as jnp
import numpy as np
from jax import lax
from jax.experimental import pallas as pl
from jax.experimental.pallas import tpu as pltpu
from jax.sharding import Mesh
from jax.sharding import PartitionSpec as P

D = 8192
H = 32
KVH = 4
HD = 128
STEPS = 4
REQ = 4
GROUPS = 16
SEQ = 16
PER_KV = H // KVH
LOCAL = 32
CONTEXT = SEQ * LOCAL
KV_WIDTH = KVH * HD
ROWS = STEPS * REQ
CHUNK = 2 * LOCAL + PER_KV * STEPS + 16

norm_eps = 1e-06
rope_base = 1000000.0
masked_score = -1e30

f32 = jnp.float32
bf16 = jnp.bfloat16


def full(shape):
    return pl.BlockSpec(shape, lambda *_: (0,) * len(shape))


def smem():
    return pl.BlockSpec(memory_space=pltpu.SMEM)


def params():
    return pltpu.CompilerParams(
        dimension_semantics=("arbitrary",), vmem_limit_bytes=48 * 1024 * 1024
    )


def wrap(value):
    return jnp.where(value >= GROUPS, value - GROUPS, value)


def project_kernel(
    slot_ref,
    shift_ref,
    group_ref,
    x_ref,
    gain_ref,
    wq_ref,
    wk_ref,
    wv_ref,
    kc_ref,
    vc_ref,
    out_ref,
    normed_ref,
    squares_ref,
):
    row8 = lax.broadcasted_iota(jnp.int32, (8, HD), 0)
    lane = lax.broadcasted_iota(jnp.int32, (8, HD), 1)

    @pl.when(pl.program_id(0) == 0)
    def _():
        tiles = []
        for r in range(REQ):
            at_group = group_ref[0]
            at_slot = jnp.int32(r)
            tile = jnp.zeros((8, HD), jnp.int32)
            for s in range(STEPS):
                leaves = slot_ref[s, at_group] == at_slot
                next_group = wrap(at_group + shift_ref[s])
                next_slot = slot_ref[s, next_group]
                at_group = jnp.where(leaves, next_group, at_group)
                at_slot = jnp.where(leaves, next_slot, at_slot)
                column = at_group * ROWS + s * REQ + at_slot
                tile = jnp.where((row8 & 3) == s, column, tile)
            tiles.append(tile)
        target = jnp.concatenate(tiles, axis=0)
        lanes = lax.broadcasted_iota(jnp.int32, (8 * REQ, HD), 1)
        x = jnp.zeros((8 * REQ, x_ref.shape[1]), f32)
        for part in range(GROUPS * ROWS // HD):
            pick = jnp.where(target == lanes + part * HD, 1.0, 0.0).astype(bf16)
            x = x + jnp.dot(
                pick, x_ref[part * HD : (part + 1) * HD, :], preferred_element_type=f32
            )
        squares_ref[...] = jnp.broadcast_to(
            jnp.sum(x * x, axis=-1, keepdims=True), squares_ref.shape
        )
        normed_ref[...] = (x * gain_ref[...].astype(f32)).astype(bf16)

    normed = normed_ref[...]
    query = jnp.dot(normed, wq_ref[...], preferred_element_type=f32)
    key = jnp.dot(normed, wk_ref[...], preferred_element_type=f32)
    value = jnp.dot(normed, wv_ref[...], preferred_element_type=f32)
    squares = squares_ref[...]
    high = squares.astype(bf16).astype(f32)
    squares = jnp.where(lax.broadcasted_iota(jnp.int32, squares.shape, 1) < HD // 2, high, squares - high)
    for r in range(REQ):
        rows = slice(r * 8, r * 8 + 8)
        tiles = [
            jnp.where(
                row8 < 4,
                query[rows, 2 * i * HD : (2 * i + 1) * HD],
                query[rows, (2 * i + 1) * HD : (2 * i + 2) * HD],
            )
            for i in range(PER_KV // 2)
        ]
        tiles.append(jnp.where(row8 < 4, key[rows], value[rows]))
        tiles.append(squares[rows])
        out_ref[r, 0:LOCAL, :] = kc_ref[r]
        out_ref[r, LOCAL : 2 * LOCAL, :] = vc_ref[r]
        out_ref[r, 2 * LOCAL : CHUNK, :] = jnp.concatenate(tiles, axis=0).astype(bf16)


def attend_kernel(len_ref, own_ref, freq_ref, in_ref, out_ref):
    length = len_ref[own_ref[0]]
    row8 = lax.broadcasted_iota(jnp.int32, (8, HD), 0)
    lane = lax.broadcasted_iota(jnp.int32, (8, HD), 1)
    total = in_ref[0, 2 * LOCAL : CHUNK, :].astype(f32)
    for k in range(1, SEQ):
        total = total + in_ref[k, 2 * LOCAL : CHUNK, :].astype(f32)
    squares = jnp.sum(total[40:48], axis=-1, keepdims=True) * (2.0 / HD)
    inverse = lax.rsqrt(squares / D + norm_eps)
    position = (length + (row8 & 3)).astype(f32)
    angles = position * freq_ref[...]
    cosine = jnp.cos(angles)
    sine = jnp.where(lane < HD // 2, -jnp.sin(angles), jnp.sin(angles))

    def rotated(tile):
        return tile * cosine + pltpu.roll(tile, HD // 2, 1) * sine

    query = jnp.concatenate(
        [rotated(total[i * 8 : i * 8 + 8] * inverse) for i in range(4)], axis=0
    ).astype(bf16)
    fresh = total[32:40] * inverse
    new_key = rotated(fresh)
    new_value = pltpu.roll(fresh, 4, 0)
    empty = jnp.zeros((HD - 8, HD), f32)
    new_key = jnp.concatenate([new_key, empty], axis=0).astype(bf16)
    new_value = jnp.concatenate([new_value, empty], axis=0).astype(bf16)

    keys = in_ref[:, 0:LOCAL, :].reshape(CONTEXT, HD)
    values = in_ref[:, LOCAL : 2 * LOCAL, :].reshape(CONTEXT, HD)
    scale = 1.0 / np.sqrt(np.float32(HD))
    contract = (((1,), (1,)), ((), ()))
    scores = lax.dot_general(query, keys, contract, preferred_element_type=f32) * scale
    recent = lax.dot_general(query, new_key, contract, preferred_element_type=f32) * scale
    column = lax.broadcasted_iota(jnp.int32, scores.shape, 1)
    scores = jnp.where(column < length, scores, masked_score)
    step = lax.broadcasted_iota(jnp.int32, recent.shape, 0) & 3
    recent = jnp.where(
        lax.broadcasted_iota(jnp.int32, recent.shape, 1) <= step, recent, masked_score
    )
    peak = jnp.maximum(
        jnp.max(scores, axis=-1, keepdims=True), jnp.max(recent, axis=-1, keepdims=True)
    )
    weights = jnp.exp(scores - peak)
    recent_weights = jnp.exp(recent - peak)
    count = jnp.sum(weights, axis=-1, keepdims=True) + jnp.sum(
        recent_weights, axis=-1, keepdims=True
    )
    summed = jnp.dot(weights.astype(bf16), values, preferred_element_type=f32) + jnp.dot(
        recent_weights.astype(bf16), new_value, preferred_element_type=f32
    )
    attention = (summed / count).astype(bf16)
    rows = attention.shape[0]
    for g in range(GROUPS):
        out_ref[g * rows : (g + 1) * rows, :] = attention


def output_kernel(slot_ref, shift_ref, group_ref, in_ref, w_ref, out_ref, attention_ref):
    @pl.when(pl.program_id(0) == 0)
    def _():
        row = lax.broadcasted_iota(jnp.int32, (2 * ROWS, HD), 0)
        lane = lax.broadcasted_iota(jnp.int32, (2 * ROWS, HD), 1)
        target = jnp.zeros((2 * ROWS, HD), jnp.int32)
        for s in range(STEPS):
            for r in range(REQ):
                at_group = group_ref[0]
                at_slot = jnp.int32(r)
                for back in range(s, -1, -1):
                    came = slot_ref[back, at_group] == at_slot
                    source = wrap(at_group - shift_ref[back] + GROUPS)
                    source_slot = slot_ref[back, source]
                    at_group = jnp.where(came, source, at_group)
                    at_slot = jnp.where(came, source_slot, at_slot)
                column = (at_group * REQ + at_slot) * 8 + s
                target = jnp.where((row & (ROWS - 1)) == s * REQ + r, column, target)
        target = target + jnp.where(row >= ROWS, 4, 0)
        picked = jnp.zeros((2 * ROWS, HD), f32)
        for part in range(in_ref.shape[0] // HD):
            pick = jnp.where(target == lane + part * HD, 1.0, 0.0).astype(bf16)
            picked = picked + jnp.dot(
                pick, in_ref[part * HD : (part + 1) * HD, :], preferred_element_type=f32
            )
        attention_ref[:, 0:HD] = picked[0:ROWS].astype(bf16)
        attention_ref[:, HD : 2 * HD] = picked[ROWS : 2 * ROWS].astype(bf16)

    projected = jnp.dot(attention_ref[...], w_ref[...], preferred_element_type=f32).astype(bf16)
    width = out_ref.shape[2]
    for k in range(out_ref.shape[0]):
        out_ref[k] = projected[:, k * width : (k + 1) * width]


def body(
    step_inputs,
    norm_gain,
    w_query,
    w_keyval,
    w_out,
    key_cache,
    value_cache,
    ctx_len,
    mig_slot,
    mig_shift,
):
    width = step_inputs.shape[2]
    group = lax.axis_index("group").astype(jnp.int32).reshape(1)
    own = lax.axis_index("seq_z").astype(jnp.int32).reshape(1)
    seq = ("seq_y", "seq_z")

    x = jnp.broadcast_to(step_inputs.reshape(1, ROWS, width), (GROUPS, ROWS, width))
    x = lax.all_to_all(x, "group", 0, 0, tiled=True).reshape(GROUPS * ROWS, width)
    heads = PER_KV * HD
    sent = pl.pallas_call(
        project_kernel,
        grid=(KVH,),
        in_specs=[
            smem(),
            smem(),
            smem(),
            full((GROUPS * ROWS, width)),
            full((1, width)),
            pl.BlockSpec((width, heads), lambda i: (0, i)),
            pl.BlockSpec((width, HD), lambda i: (0, i)),
            pl.BlockSpec((width, HD), lambda i: (0, KVH + i)),
            pl.BlockSpec((REQ, LOCAL, HD), lambda i: (0, 0, i)),
            pl.BlockSpec((REQ, LOCAL, HD), lambda i: (0, 0, i)),
        ],
        out_specs=pl.BlockSpec((REQ, CHUNK, HD), lambda i: (i, 0, 0)),
        out_shape=jax.ShapeDtypeStruct((SEQ, CHUNK, HD), bf16),
        scratch_shapes=[pltpu.VMEM((8 * REQ, width), bf16), pltpu.VMEM((8 * REQ, HD), f32)],
        compiler_params=params(),
        name="project",
    )(
        mig_slot,
        mig_shift,
        group,
        x,
        norm_gain.reshape(1, width),
        w_query,
        w_keyval,
        w_keyval,
        key_cache,
        value_cache,
    )
    received = lax.all_to_all(sent, seq, 0, 0, tiled=True)

    half = np.arange(HD) % (HD // 2)
    freq = jnp.asarray((rope_base ** (-2.0 * half / HD)).astype(np.float32).reshape(1, HD))
    attention = pl.pallas_call(
        attend_kernel,
        grid=(1,),
        in_specs=[smem(), smem(), full((1, HD)), full((SEQ, CHUNK, HD))],
        out_specs=full((GROUPS * PER_KV * STEPS, HD)),
        out_shape=jax.ShapeDtypeStruct((GROUPS * PER_KV * STEPS, HD), bf16),
        compiler_params=params(),
        name="attend",
    )(ctx_len, own, freq, received)
    attention = lax.all_to_all(
        attention.reshape(GROUPS * 4, 8, HD), ("group", "seq_z"), 0, 0, tiled=True
    ).reshape(GROUPS * 4 * 8, HD)

    blocks = 4
    shares = pl.pallas_call(
        output_kernel,
        grid=(blocks,),
        in_specs=[
            smem(),
            smem(),
            smem(),
            full((GROUPS * 4 * 8, HD)),
            pl.BlockSpec((2 * HD, D // blocks), lambda i: (0, i)),
        ],
        out_specs=pl.BlockSpec((SEQ // blocks, ROWS, width), lambda i: (i, 0, 0)),
        out_shape=jax.ShapeDtypeStruct((SEQ, ROWS, width), bf16),
        scratch_shapes=[pltpu.VMEM((ROWS, 2 * HD), bf16)],
        compiler_params=params(),
        name="output",
    )(mig_slot, mig_shift, group, attention, w_out)
    shares = lax.all_to_all(shares, seq, 0, 0, tiled=True)
    result = jnp.sum(shares.astype(f32), axis=0).astype(bf16)
    return result.reshape(STEPS, REQ, width)


def solution(mesh):
    split = Mesh(mesh.devices.reshape(GROUPS, 4, 4), ("group", "seq_y", "seq_z"))
    seq = ("seq_y", "seq_z")
    placed = (
        P(None, "group", seq),
        P(seq),
        P(seq, None),
        P(seq, None),
        P(seq, None),
        P("group", seq, None),
        P("group", seq, None),
        P("group"),
        P(),
        P(),
    )
    return jax.shard_map(
        body, mesh=split, in_specs=placed, out_specs=P(None, "group", seq), check_vma=False
    )
```

time: 1360 us -> 90.2 us (0.07)
  blocking collectives: 764 us -> 31.6 us
  waiting for transfers between devices: 488 us -> 23.8 us
  matrix products: 29.1 us -> 0 us
  other arithmetic: 27.5 us -> 0.04 us
  between operations: 24.9 us -> 0.06 us
  starting transfers between devices: 0.21 us -> 16.1 us
  local copies, waits for them, and re-layouts: 25 us -> 9.34 us
    all_gather x26 -> x0, blocking collectives: 752 us -> none  [the longest x12 488 us: merged(): lax.all_gather(part.astype(kind), axis)]
    unnamed x10 -> x0, waiting for transfers between devices: 334 us -> none
    psum x2 -> x0, waiting for transfers between devices: 155 us -> none  [body(): lax.psum((square_part, query_part, keyval_part), 'seq')]
    all_to_all x0 -> x2, blocking collectives: none -> 31.6 us  [the longest x1 16.7 us: body(): shares = lax.all_to_all(shares, seq, 0, 0, tiled=True)]
    dot_general x28 -> x0, matrix products: 29.1 us -> none  [the longest x4 11.4 us: body(): projected = jnp.dot(attention, w_out, preferred_element_type=jnp.float32)]
    all_to_all x0 -> x2, waiting for transfers between devices: none -> 23.8 us  [the longest x1 17.7 us: body(): received = lax.all_to_all(sent, seq, 0, 0, tiled=True)]
    all_to_all x0 -> x2, starting transfers between devices: none -> 16.1 us  [the longest x1 10.3 us: body(): received = lax.all_to_all(sent, seq, 0, 0, tiled=True)]
  transfers between devices with their start and end apart: 6 -> 2, of which waited for: 6 -> 2; matrix products, arithmetic and copies ran while one was open for 3% -> 1% of each run, Pallas kernels for 0% -> 0%
where the time goes in v1:
time: 90.2 us; the launch traced here: 88.9 us
  blocking collectives  31.6 us (35%)
  waiting for transfers between devices  23.8 us (26%)
  starting transfers between devices  16.1 us (18%)
  local copies, waits for them, and re-layouts  9.34 us (10%)
  Pallas kernels  8.03 us (9%)
    all_to_all x1, waiting for transfers between devices, body(): received = lax.all_to_all(sent, seq, 0, 0, tiled=True)  17.7 us
    all_to_all x1, blocking collectives, body(): shares = lax.all_to_all(shares, seq, 0, 0, tiled=True)  16.7 us
    all_to_all x1, blocking collectives, body(): lax.all_to_all(attention.reshape(GROUPS * 4, 8, HD), ('group', 'seq_z'),...  14.9 us
    all_to_all x1, starting transfers between devices, body(): received = lax.all_to_all(sent, seq, 0, 0, tiled=True)  10.3 us
    unnamed x20, local copies, waits for them, and re-layouts  6.57 us
    all_to_all x1, waiting for transfers between devices, body(): lax.all_to_all(x, 'group', 0, 0, tiled=True).reshape(GROUPS * ROWS, width)  6.07 us
    all_to_all x1, starting transfers between devices, body(): lax.all_to_all(x, 'group', 0, 0, tiled=True).reshape(GROUPS * ROWS, width)  5.77 us
    pallas_call x1, Pallas kernels, body(): pl.pallas_call(project_kernel, grid=(KVH,), in_specs=[smem(), smem(), sme...  4.84 us
  transfers between devices with their start and end apart: 2, of which 2 were waited for; matrix products, arithmetic and copies ran while one was open for 1% of the time, Pallas kernels for 0%

profile of v1, /device:TPU:32, one launch (start us, length us, event | category | flops | bytes accessed | tf_op | source)
XLA Modules:
  0.0 88.9 jit_solution(229578113485105584)
XLA Ops:
  0.0 0.7 broadcast_in_dim.7
  0.7 0.7 broadcast_in_dim.8
  1.5 5.8 %all-to-all-start = ((bf16[16,16,512]{2,1,0:T(8,128)(2,1)}), bf16[16,16,512]{2,1,0:T(8,128)(2,1)S(1)}, u32[]{:S(2)}, u32[]{:S(2)}) async-start(bf16[16,16,512]{2,1,0:T(8,128)(2,1)} %broadcast_in_dim.8), calls=%async_computation | async-start | bytes 524288 | tf_op jit(solution)/shard_map/all_to_all | solution.py:232
  7.2 0.0 copy-start.9
  7.3 0.7 reshape.26.gain_ref
  8.0 6.1 %all-to-all-done = bf16[16,16,512]{2,1,0:T(8,128)(2,1)S(1)} async-done(((bf16[16,16,512]{2,1,0:T(8,128)(2,1)}), bf16[16,16,512]{2,1,0:T(8,128)(2,1)S(1)}, u32[]{:S(2)}, u32[]{:S(2)}) %all-to-all-start) | async-done | bytes 262176 | tf_op jit(solution)/shard_map/all_to_all | solution.py:232
  14.0 1.2 %copy-done = bf16[512,1024]{1,0:T(8,128)(2,1)S(1)} copy-done((bf16[512,1024]{1,0:T(8,128)(2,1)S(1)}, bf16[512,1024]{1,0:T(8,128)(2,1)}, u32[]{:S(2)}) %copy-start) | copy-done | bytes 1048600
  15.3 0.9 %copy-done.2 = bf16[4,32,512]{2,1,0:T(8,128)(2,1)S(1)} copy-done((bf16[4,32,512]{2,1,0:T(8,128)(2,1)S(1)}, bf16[4,32,512]{2,1,0:T(8,128)(2,1)}, u32[]{:S(2)}) %copy-start.2) | copy-done | bytes 131096
  16.2 0.9 %copy-done.3 = bf16[4,32,512]{2,1,0:T(8,128)(2,1)S(1)} copy-done((bf16[4,32,512]{2,1,0:T(8,128)(2,1)S(1)}, bf16[4,32,512]{2,1,0:T(8,128)(2,1)}, u32[]{:S(2)}) %copy-start.3) | copy-done | bytes 131096
  17.1 0.7 copy-done.4
  17.7 0.7 copy-done.6
  18.4 4.8 %project.1 = bf16[16,112,128]{2,1,0:T(8,128)(2,1)} custom-call(s32[4,16]{1,0:T(4,128)S(1)} %copy-done.4, s32[4]{0:T(128)S(1)} %copy-done.6, s32[1]{0:T(128)} %bitcast.group_ref, bf16[256,512]{1,0:T(8,128)(2,1)S(1)} %bitcast.5, bf16[1,512]{1,0:T(2,128)(2,1)S(1)} %reshape.26.gain_ref, bf16[512,4096]{1,0:T(8,128)(2,1)} %wq_ref.1, ...), custom_call_target="tpu_custom_call" | custom-call | tf_op jit(solution)/shard_map/project/pallas_call | solution.py:234
  23.2 10.3 %all-to-all-start.1 = ((bf16[16,112,128]{2,1,0:T(8,128)(2,1)}), bf16[16,112,128]{2,1,0:T(8,128)(2,1)S(1)}, u32[]{:S(2)}, u32[]{:S(2)}) async-start(bf16[16,112,128]{2,1,0:T(8,128)(2,1)} %project.1), calls=%async_computation.1 | async-start | bytes 917504 | tf_op jit(solution)/shard_map/all_to_all | solution.py:266
  33.6 17.7 %all-to-all-done.1.in_ref = bf16[16,112,128]{2,1,0:T(8,128)(2,1)S(1)} async-done(((bf16[16,112,128]{2,1,0:T(8,128)(2,1)}), bf16[16,112,128]{2,1,0:T(8,128)(2,1)S(1)}, u32[]{:S(2)}, u32[]{:S(2)}) %all-to-all-start.1) | async-done | bytes 458784 | tf_op jit(solution)/shard_map/all_to_all | solution.py:266
  51.3 0.0 copy-done.8
  51.3 0.0 copy-done.9
  51.3 1.1 %attend.1 = bf16[512,128]{1,0:T(8,128)(2,1)S(1)} custom-call(s32[4]{0:T(128)S(1)} %copy-done.8, s32[1]{0:T(128)} %bitcast.1.own_ref, f32[1,128]{1,0:T(1,128)S(1)} %copy-done.9, bf16[16,112,128]{2,1,0:T(8,128)(2,1)S(1)} %all-to-all-done.1.in_ref), custom_call_target="tpu_custom_call" | custom-call | tf_op jit(solution)/shard_map/attend/pallas_call | solution.py:270
  52.3 14.9 %all_to_all.20 = bf16[64,8,128]{2,1,0:T(8,128)(2,1)S(1)} all-to-all(bf16[64,8,128]{2,1,0:T(8,128)(2,1)S(1)} %bitcast.7), channel_id=1, replica_groups=mesh['group'=16,'seq_y'=4,'seq_z'=4] {'group','seq_z'}, dimensions={0} | all-to-all | bytes 262144 | tf_op jit(solution)/shard_map/all_to_all | solution.py:279
  67.2 0.0 copy-done.5
  67.2 0.0 copy-done.7
  67.2 2.2 %copy-done.1 = bf16[256,8192]{1,0:T(8,128)(2,1)S(1)} copy-done((bf16[256,8192]{1,0:T(8,128)(2,1)S(1)}, bf16[256,8192]{1,0:T(8,128)(2,1)}, u32[]{:S(2)}) %copy-start.1) | copy-done | bytes 4194328
  69.4 2.1 %output.1 = bf16[16,16,512]{2,1,0:T(8,128)(2,1)S(1)} custom-call(s32[4,16]{1,0:T(4,128)S(1)} %copy-done.5, s32[4]{0:T(128)S(1)} %copy-done.7, s32[1]{0:T(128)} %bitcast.group_ref, bf16[512,128]{1,0:T(8,128)(2,1)S(1)} %bitcast.6, bf16[256,8192]{1,0:T(8,128)(2,1)S(1)} %copy-done.1), custom_call_target="tpu_custom_call" | custom-call | tf_op jit(solution)/shard_map/output/pallas_call | solution.py:284
  71.5 16.7 %all_to_all.21 = bf16[16,16,512]{2,1,0:T(8,128)(2,1)S(1)} all-to-all(bf16[16,16,512]{2,1,0:T(8,128)(2,1)S(1)} %output.1), channel_id=1, replica_groups=mesh['group'=16,'seq_y'=4,'seq_z'=4] {'seq_y','seq_z'}, dimensions={0} | all-to-all | bytes 524288 | tf_op jit(solution)/shard_map/all_to_all | solution.py:300
  88.3 0.6 reshape.29
  (10 shorter events, 0.1 us)
Async XLA Ops:
  1.5 12.6 %all-to-all-start = ((bf16[16,16,512]{2,1,0:T(8,128)(2,1)}), bf16[16,16,512]{2,1,0:T(8,128)(2,1)S(1)}, u32[]{:S(2)}, u32[]{:S(2)}) async-start(bf16[16,16,512]{2,1,0:T(8,128)(2,1)} %broadcast_in_dim.8), calls=%async_computation | async-start | bytes 524288 | tf_op jit(solution)/shard_map/all_to_all | solution.py:232
  7.2 44.0 %copy-start.8 = (s32[4]{0:T(128)S(1)}, s32[4]{0:T(128)}, u32[]{:S(2)}) copy-start(s32[4]{0:T(128)} %len_ref.1) | copy-start | bytes 52
  7.2 44.0 %copy-start.9 = (f32[1,128]{1,0:T(1,128)S(1)}, f32[1,128]{1,0:T(1,128)}, u32[]{:S(2)}) copy-start(f32[1,128]{1,0:T(1,128)} %constant.14.clone.freq_ref) | copy-start | bytes 1540
  14.0 1.2 %copy-start = (bf16[512,1024]{1,0:T(8,128)(2,1)S(1)}, bf16[512,1024]{1,0:T(8,128)(2,1)}, u32[]{:S(2)}) copy-start(bf16[512,1024]{1,0:T(8,128)(2,1)} %wv_ref.1) | copy-start | bytes 3145732
  15.3 0.9 %copy-start.2 = (bf16[4,32,512]{2,1,0:T(8,128)(2,1)S(1)}, bf16[4,32,512]{2,1,0:T(8,128)(2,1)}, u32[]{:S(2)}) copy-start(bf16[4,32,512]{2,1,0:T(8,128)(2,1)} %kc_ref.1) | copy-start | bytes 393220
  16.2 0.9 %copy-start.3 = (bf16[4,32,512]{2,1,0:T(8,128)(2,1)S(1)}, bf16[4,32,512]{2,1,0:T(8,128)(2,1)}, u32[]{:S(2)}) copy-start(bf16[4,32,512]{2,1,0:T(8,128)(2,1)} %vc_ref.1) | copy-start | bytes 393220
  17.1 0.7 copy-start.4
  17.7 0.7 copy-start.6
  18.4 48.8 %copy-start.5 = (s32[4,16]{1,0:T(4,128)S(1)}, s32[4,16]{1,0:T(4,128)}, u32[]{:S(2)}) copy-start(s32[4,16]{1,0:T(4,128)} %slot_ref.3) | copy-start | bytes 772
  18.4 48.8 %copy-start.7 = (s32[4]{0:T(128)S(1)}, s32[4]{0:T(128)}, u32[]{:S(2)}) copy-start(s32[4]{0:T(128)} %shift_ref.3) | copy-start | bytes 52
  23.2 28.0 %all-to-all-start.1 = ((bf16[16,112,128]{2,1,0:T(8,128)(2,1)}), bf16[16,112,128]{2,1,0:T(8,128)(2,1)S(1)}, u32[]{:S(2)}, u32[]{:S(2)}) async-start(bf16[16,112,128]{2,1,0:T(8,128)(2,1)} %project.1), calls=%async_computation.1 | async-start | bytes 917504 | tf_op jit(solution)/shard_map/all_to_all | solution.py:266
  67.2 2.2 %copy-start.1 = (bf16[256,8192]{1,0:T(8,128)(2,1)S(1)}, bf16[256,8192]{1,0:T(8,128)(2,1)}, u32[]{:S(2)}) copy-start(bf16[256,8192]{1,0:T(8,128)(2,1)} %w_ref.1) | copy-start | bytes 12582916

commit v2 on v1

v2 whole, which is shorter than its diff:
```python
import jax
import jax.numpy as jnp
import numpy as np
from jax import lax
from jax.experimental import pallas as pl
from jax.experimental.pallas import tpu as pltpu
from jax.sharding import Mesh
from jax.sharding import PartitionSpec as P

D = 8192
H = 32
KVH = 4
HD = 128
STEPS = 4
REQ = 4
GROUPS = 16
SEQ = 16
PER_KV = H // KVH
LOCAL = 32
CONTEXT = SEQ * LOCAL
KV_WIDTH = KVH * HD
ROWS = STEPS * REQ
CHUNK = 2 * LOCAL + PER_KV * STEPS + 16

norm_eps = 1e-06
rope_base = 1000000.0
masked_score = -1e30

f32 = jnp.float32
bf16 = jnp.bfloat16


def anywhere():
    return pl.BlockSpec(memory_space=pl.ANY)


def in_vmem():
    return pl.BlockSpec(memory_space=pltpu.VMEM)


def params(mib=16):
    return pltpu.CompilerParams(vmem_limit_bytes=mib * 1024 * 1024)


def placed(array):
    return pltpu.with_memory_space_constraint(array, pltpu.VMEM)


def left(array):
    return pltpu.with_memory_space_constraint(array, pltpu.HBM)


def wrap(value):
    return jnp.where(value >= GROUPS, value - GROUPS, value)


def spread_kernel(x_hbm, out_ref, x_ref, sem):
    copy = pltpu.make_async_copy(x_hbm, x_ref, sem)
    copy.start()
    copy.wait()
    x = jnp.concatenate([x_ref[s].astype(f32) for s in range(STEPS)], axis=0).astype(bf16)
    for g in range(GROUPS):
        out_ref[g] = x


def prepare_kernel(
    slot_hbm,
    shift_hbm,
    len_hbm,
    group_ref,
    own_ref,
    freq_hbm,
    wq_hbm,
    wkv_hbm,
    kc_hbm,
    vc_hbm,
    pick_in_ref,
    pick_out_ref,
    table_ref,
    wkv_ref,
    kc_ref,
    vc_ref,
    wq0_ref,
    slot_ref,
    shift_ref,
    len_ref,
    freq_ref,
    sems,
):
    small = [
        pltpu.make_async_copy(slot_hbm, slot_ref, sems.at[0]),
        pltpu.make_async_copy(shift_hbm, shift_ref, sems.at[1]),
        pltpu.make_async_copy(len_hbm, len_ref, sems.at[2]),
        pltpu.make_async_copy(freq_hbm, freq_ref, sems.at[7]),
    ]
    large = [
        pltpu.make_async_copy(kc_hbm, kc_ref, sems.at[3]),
        pltpu.make_async_copy(vc_hbm, vc_ref, sems.at[4]),
        pltpu.make_async_copy(wkv_hbm, wkv_ref, sems.at[5]),
    ]
    columns = pl.ds(0, wq0_ref.shape[1])
    large.append(pltpu.make_async_copy(wq_hbm.at[:, columns], wq0_ref, sems.at[6]))
    for copy in small + large:
        copy.start()
    for copy in small:
        copy.wait()
    group = group_ref[0]
    own = own_ref[0]

    row8 = lax.broadcasted_iota(jnp.int32, (8, HD), 0)
    lane = lax.broadcasted_iota(jnp.int32, (8, HD), 1)
    for r in range(REQ):
        at_group = group
        at_slot = jnp.int32(r)
        target = jnp.zeros((8, HD), jnp.int32)
        for s in range(STEPS):
            leaves = slot_ref[s, at_group] == at_slot
            next_group = wrap(at_group + shift_ref[s])
            next_slot = slot_ref[s, next_group]
            at_group = jnp.where(leaves, next_group, at_group)
            at_slot = jnp.where(leaves, next_slot, at_slot)
            column = at_group * ROWS + s * REQ + at_slot
            target = jnp.where((row8 & 3) == s, column, target)
        for part in range(GROUPS * ROWS // HD):
            pick_in_ref[r * 8 : r * 8 + 8, part * HD : (part + 1) * HD] = jnp.where(
                target == lane + part * HD, 1.0, 0.0
            )

    row = lax.broadcasted_iota(jnp.int32, (2 * ROWS, HD), 0)
    lanes = lax.broadcasted_iota(jnp.int32, (2 * ROWS, HD), 1)
    target = jnp.zeros((2 * ROWS, HD), jnp.int32)
    for s in range(STEPS):
        for r in range(REQ):
            at_group = group
            at_slot = jnp.int32(r)
            for back in range(s, -1, -1):
                came = slot_ref[back, at_group] == at_slot
                source = wrap(at_group - shift_ref[back] + GROUPS)
                source_slot = slot_ref[back, source]
                at_group = jnp.where(came, source, at_group)
                at_slot = jnp.where(came, source_slot, at_slot)
            column = (at_group * REQ + at_slot) * 8 + s
            target = jnp.where((row & (ROWS - 1)) == s * REQ + r, column, target)
    target = target + jnp.where(row >= ROWS, 4, 0)
    for part in range(GROUPS * REQ * 8 // HD):
        pick_out_ref[:, part * HD : (part + 1) * HD] = jnp.where(
            target == lanes + part * HD, 1.0, 0.0
        ).astype(bf16)

    length = len_ref[own]
    angles = (length + (row8 & 3)).astype(f32) * freq_ref[...]
    sine = jnp.sin(angles)
    table_ref[:, 0:HD] = jnp.cos(angles)
    table_ref[:, HD : 2 * HD] = jnp.where(lane < HD // 2, -sine, sine)
    for part in range(CONTEXT // HD):
        table_ref[:, (2 + part) * HD : (3 + part) * HD] = jnp.where(
            lane + part * HD < length, 1.0, 0.0
        )
    for copy in large:
        copy.wait()


def project_kernel(
    x_ref,
    pick_ref,
    gain_ref,
    wkv_ref,
    kc_ref,
    vc_ref,
    wq0_ref,
    wq_hbm,
    out_ref,
    wq1_ref,
    wq2_ref,
    wq3_ref,
    sems,
):
    copies = []
    for k, part in enumerate((wq1_ref, wq2_ref, wq3_ref)):
        columns = pl.ds((1 + k) * part.shape[1], part.shape[1])
        copies.append(pltpu.make_async_copy(wq_hbm.at[:, columns], part, sems.at[k]))
        copies[k].start(priority=1)
    row8 = lax.broadcasted_iota(jnp.int32, (8, HD), 0)
    x = jnp.dot(pick_ref[...].astype(bf16), x_ref[...], preferred_element_type=f32)
    squares = jnp.sum(x * x, axis=-1, keepdims=True)
    normed = (x * gain_ref[...].astype(f32)).astype(bf16)
    squares = jnp.broadcast_to(squares, (8 * REQ, HD))
    high = squares.astype(bf16).astype(f32)
    lanes = lax.broadcasted_iota(jnp.int32, squares.shape, 1)
    squares = jnp.where(lanes < HD // 2, high, squares - high)
    for k, wq_ref in enumerate((wq0_ref, wq1_ref, wq2_ref, wq3_ref)):
        if k >= 1:
            copies[k - 1].wait()
        query = jnp.dot(normed, wq_ref[...], preferred_element_type=f32)
        key = jnp.dot(normed, wkv_ref[:, k * HD : (k + 1) * HD], preferred_element_type=f32)
        value = jnp.dot(
            normed,
            wkv_ref[:, KV_WIDTH + k * HD : KV_WIDTH + (k + 1) * HD],
            preferred_element_type=f32,
        )
        for r in range(REQ):
            rows = slice(r * 8, r * 8 + 8)
            tiles = [
                jnp.where(
                    row8 < 4,
                    query[rows, 2 * i * HD : (2 * i + 1) * HD],
                    query[rows, (2 * i + 1) * HD : (2 * i + 2) * HD],
                )
                for i in range(PER_KV // 2)
            ]
            tiles.append(jnp.where(row8 < 4, key[rows], value[rows]))
            tiles.append(squares[rows])
            at = k * REQ + r
            out_ref[at, 0:LOCAL, :] = kc_ref[r, :, k * HD : (k + 1) * HD]
            out_ref[at, LOCAL : 2 * LOCAL, :] = vc_ref[r, :, k * HD : (k + 1) * HD]
            out_ref[at, 2 * LOCAL : CHUNK, :] = jnp.concatenate(tiles, axis=0).astype(bf16)


def attend_kernel(table_ref, in_ref, out_ref):
    total = in_ref[0, 2 * LOCAL : CHUNK, :].astype(f32)
    for k in range(1, SEQ):
        total = total + in_ref[k, 2 * LOCAL : CHUNK, :].astype(f32)
    squares = jnp.sum(total[40:48], axis=-1, keepdims=True) * (2.0 / HD)
    inverse = lax.rsqrt(squares / D + norm_eps)
    cosine = table_ref[:, 0:HD]
    sine = table_ref[:, HD : 2 * HD]

    def rotated(tile):
        return tile * cosine + pltpu.roll(tile, HD // 2, 1) * sine

    query = jnp.concatenate(
        [rotated(total[i * 8 : i * 8 + 8] * inverse) for i in range(4)], axis=0
    ).astype(bf16)
    fresh = total[32:40] * inverse
    new_key = rotated(fresh)
    new_value = pltpu.roll(fresh, 4, 0)
    empty = jnp.zeros((HD - 8, HD), f32)
    new_key = jnp.concatenate([new_key, empty], axis=0).astype(bf16)
    new_value = jnp.concatenate([new_value, empty], axis=0).astype(bf16)

    keys = in_ref[:, 0:LOCAL, :].reshape(CONTEXT, HD)
    values = in_ref[:, LOCAL : 2 * LOCAL, :].reshape(CONTEXT, HD)
    scale = 1.0 / np.sqrt(np.float32(HD))
    contract = (((1,), (1,)), ((), ()))
    scores = lax.dot_general(query, keys, contract, preferred_element_type=f32) * scale
    recent = lax.dot_general(query, new_key, contract, preferred_element_type=f32) * scale
    live = jnp.broadcast_to(table_ref[0:1, 2 * HD : 2 * HD + CONTEXT], scores.shape)
    scores = jnp.where(live > 0.5, scores, masked_score)
    step = lax.broadcasted_iota(jnp.int32, recent.shape, 0) & 3
    recent = jnp.where(
        lax.broadcasted_iota(jnp.int32, recent.shape, 1) <= step, recent, masked_score
    )
    peak = jnp.maximum(
        jnp.max(scores, axis=-1, keepdims=True), jnp.max(recent, axis=-1, keepdims=True)
    )
    weights = jnp.exp(scores - peak)
    recent_weights = jnp.exp(recent - peak)
    count = jnp.sum(weights, axis=-1, keepdims=True) + jnp.sum(
        recent_weights, axis=-1, keepdims=True
    )
    summed = jnp.dot(weights.astype(bf16), values, preferred_element_type=f32) + jnp.dot(
        recent_weights.astype(bf16), new_value, preferred_element_type=f32
    )
    attention = (summed / count).astype(bf16)
    rows = attention.shape[0]
    for g in range(GROUPS):
        out_ref[g * rows : (g + 1) * rows, :] = attention


def output_kernel(pick_ref, in_ref, w_ref, out_ref):
    picked = jnp.dot(pick_ref[...], in_ref[...], preferred_element_type=f32)
    attention = jnp.concatenate([picked[0:ROWS], picked[ROWS : 2 * ROWS]], axis=1).astype(bf16)
    width = out_ref.shape[2]
    for k in range(SEQ):
        columns = slice(k * width, (k + 1) * width)
        out_ref[k] = jnp.dot(
            attention, w_ref[:, columns], preferred_element_type=f32
        ).astype(bf16)


def gather_kernel(in_ref, out_ref):
    total = in_ref[0].astype(f32)
    for k in range(1, SEQ):
        total = total + in_ref[k].astype(f32)
    for s in range(STEPS):
        out_ref[s] = total[s * REQ : (s + 1) * REQ].astype(bf16)


def body(
    step_inputs,
    norm_gain,
    w_query,
    w_keyval,
    w_out,
    key_cache,
    value_cache,
    ctx_len,
    mig_slot,
    mig_shift,
):
    width = step_inputs.shape[2]
    seq = ("seq_y", "seq_z")
    group = lax.axis_index("group").astype(jnp.int32).reshape(1)
    own = lax.axis_index("seq_z").astype(jnp.int32).reshape(1)

    x = pl.pallas_call(
        spread_kernel,
        in_specs=[anywhere()],
        out_specs=in_vmem(),
        out_shape=jax.ShapeDtypeStruct((GROUPS, ROWS, width), bf16),
        scratch_shapes=[pltpu.VMEM(step_inputs.shape, bf16), pltpu.SemaphoreType.DMA],
        compiler_params=params(),
        name="spread",
    )(left(step_inputs))
    x = lax.all_to_all(x, "group", 0, 0, tiled=True).reshape(GROUPS * ROWS, width)

    half = np.arange(HD) % (HD // 2)
    freq = jnp.asarray((rope_base ** (-2.0 * half / HD)).astype(np.float32).reshape(1, HD))
    large = (w_query, w_keyval, key_cache, value_cache)
    pick_in, pick_out, table, wkv, kc, vc, *split = pl.pallas_call(
        prepare_kernel,
        in_specs=[anywhere()] * 3
        + [pl.BlockSpec(memory_space=pltpu.SMEM)] * 2
        + [anywhere()] * 5,
        out_specs=[in_vmem()] * 7,
        out_shape=[
            pltpu.VMEM((8 * REQ, GROUPS * ROWS), f32),
            pltpu.VMEM((2 * ROWS, GROUPS * REQ * 8), bf16),
            pltpu.VMEM((8, 2 * HD + CONTEXT), f32),
        ]
        + [pltpu.VMEM(array.shape, bf16) for array in (w_keyval, key_cache, value_cache)]
        + [pltpu.VMEM((width, PER_KV * HD), bf16)],
        scratch_shapes=[
            pltpu.SMEM(mig_slot.shape, jnp.int32),
            pltpu.SMEM(mig_shift.shape, jnp.int32),
            pltpu.SMEM(ctx_len.shape, jnp.int32),
            pltpu.VMEM((1, HD), f32),
            pltpu.SemaphoreType.DMA((8,)),
        ],
        compiler_params=params(),
        cost_estimate=pl.CostEstimate(flops=0, bytes_accessed=20_000_000, transcendentals=0),
        name="prepare",
    )(
        left(mig_slot),
        left(mig_shift),
        left(ctx_len),
        group,
        own,
        left(freq),
        *[left(array) for array in large],
    )

    sent = pl.pallas_call(
        project_kernel,
        in_specs=[in_vmem()] * 7 + [anywhere()],
        out_specs=in_vmem(),
        out_shape=jax.ShapeDtypeStruct((SEQ, CHUNK, HD), bf16),
        scratch_shapes=[pltpu.VMEM((width, PER_KV * HD), bf16)] * 3
        + [pltpu.SemaphoreType.DMA((3,))],
        compiler_params=params(),
        name="project",
    )(
        x,
        placed(pick_in),
        norm_gain.reshape(1, width),
        placed(wkv),
        placed(kc),
        placed(vc),
        *[placed(part) for part in split],
        left(w_query),
    )
    received = lax.all_to_all(sent, seq, 0, 0, tiled=True)

    attention = pl.pallas_call(
        attend_kernel,
        in_specs=[in_vmem()] * 2,
        out_specs=in_vmem(),
        out_shape=jax.ShapeDtypeStruct((GROUPS * PER_KV * STEPS, HD), bf16),
        compiler_params=params(),
        name="attend",
    )(placed(table), received)
    attention = lax.all_to_all(
        attention.reshape(GROUPS * 4, 8, HD), ("group", "seq_z"), 0, 0, tiled=True
    ).reshape(GROUPS * 4 * 8, HD)

    shares = pl.pallas_call(
        output_kernel,
        in_specs=[in_vmem()] * 3,
        out_specs=in_vmem(),
        out_shape=jax.ShapeDtypeStruct((SEQ, ROWS, width), bf16),
        compiler_params=params(),
        name="output",
    )(placed(pick_out), attention, placed(w_out))
    shares = lax.all_to_all(shares, seq, 0, 0, tiled=True)
    return pl.pallas_call(
        gather_kernel,
        in_specs=[in_vmem()],
        out_specs=in_vmem(),
        out_shape=jax.ShapeDtypeStruct((STEPS, REQ, width), bf16),
        compiler_params=params(),
        name="gather",
    )(shares)


def solution(mesh):
    split = Mesh(mesh.devices.reshape(GROUPS, 4, 4), ("group", "seq_y", "seq_z"))
    seq = ("seq_y", "seq_z")
    specs = (
        P(None, "group", seq),
        P(seq),
        P(seq, None),
        P(seq, None),
        P(seq, None),
        P("group", seq, None),
        P("group", seq, None),
        P("group"),
        P(),
        P(),
    )
    return jax.shard_map(
        body, mesh=split, in_specs=specs, out_specs=P(None, "group", seq), check_vma=False
    )
```

time: 90.2 us -> 78.9 us (0.87)
  blocking collectives: 31.6 us -> 59.4 us
  waiting for transfers between devices: 23.8 us -> 4.33 us
  starting transfers between devices: 16.1 us -> 5.79 us
  local copies, waits for them, and re-layouts: 9.34 us -> 0.69 us
    all_to_all x0 -> x1, blocking collectives: none -> 27.8 us  [body(): received = lax.all_to_all(sent, seq, 0, 0, tiled=True)]
    all_to_all x1 -> x0, waiting for transfers between devices: 17.7 us -> none  [body(): received = lax.all_to_all(sent, seq, 0, 0, tiled=True)]
    all_to_all x1 -> x0, starting transfers between devices: 10.3 us -> none  [body(): received = lax.all_to_all(sent, seq, 0, 0, tiled=True)]
    unnamed x20 -> x2, local copies, waits for them, and re-layouts: 6.57 us -> 0.01 us
    all_to_all x1, waiting for transfers between devices: 6.07 us -> 4.33 us  [body(): lax.all_to_all(x, 'group', 0, 0, tiled=True).reshape(GROUPS * ROWS, width)]
    broadcast_in_dim x2 -> x0, local copies, waits for them, and re-layouts: 1.46 us -> none  [body(): jnp.broadcast_to(step_inputs.reshape(1, ROWS, width), (GROUPS, ROWS, width))]
    pallas_call x3 -> x6, Pallas kernels: 8.03 us -> 7.63 us  [the longest x1 2.48 us: body(): pl.pallas_call(project_kernel, in_specs=[in_vmem()] * 7 + [anywhere()], o...]
  transfers between devices with their start and end apart: 2 -> 1, of which waited for: 2 -> 1; matrix products, arithmetic and copies ran while one was open for 1% -> 1% of each run, Pallas kernels for 0% -> 2%
where the time goes in v2:
time: 78.9 us; the launch traced here: 77.8 us
  blocking collectives  59.4 us (75%)
  Pallas kernels  7.63 us (10%)
  starting transfers between devices  5.79 us (7%)
  waiting for transfers between devices  4.33 us (5%)
    all_to_all x1, blocking collectives, body(): received = lax.all_to_all(sent, seq, 0, 0, tiled=True)  27.8 us
    all_to_all x1, blocking collectives, body(): shares = lax.all_to_all(shares, seq, 0, 0, tiled=True)  16.7 us
    all_to_all x1, blocking collectives, body(): lax.all_to_all(attention.reshape(GROUPS * 4, 8, HD), ('group', 'seq_z'),...  14.9 us
    all_to_all x1, starting transfers between devices, body(): lax.all_to_all(x, 'group', 0, 0, tiled=True).reshape(GROUPS * ROWS, width)  5.79 us
    all_to_all x1, waiting for transfers between devices, body(): lax.all_to_all(x, 'group', 0, 0, tiled=True).reshape(GROUPS * ROWS, width)  4.33 us
    pallas_call x1, Pallas kernels, body(): pl.pallas_call(project_kernel, in_specs=[in_vmem()] * 7 + [anywhere()], o...  2.48 us
    pallas_call x1, Pallas kernels, body(): pl.pallas_call(prepare_kernel, in_specs=[anywhere()] * 3 + [pl.BlockSpec(...  1.76 us
  transfers between devices with their start and end apart: 1, of which 1 were waited for; matrix products, arithmetic and copies ran while one was open for 1% of the time, Pallas kernels for 2%

profile of v2, /device:TPU:32, one launch (start us, length us, event | category | flops | bytes accessed | tf_op | source)
XLA Modules:
  0.0 77.8 jit_solution(8056275783797894265)
XLA Ops:
  0.0 1.4 %spread.1 = bf16[16,16,512]{2,1,0:T(8,128)(2,1)} custom-call(bf16[4,4,512]{2,1,0:T(4,128)(2,1)} %x_hbm.1), custom_call_target="tpu_custom_call" | custom-call | tf_op jit(solution)/shard_map/spread/pallas_call | solution.py:306
  1.5 5.8 %all-to-all-start = ((bf16[16,16,512]{2,1,0:T(8,128)(2,1)}), bf16[16,16,512]{2,1,0:T(8,128)(2,1)S(1)}, u32[]{:S(2)}, u32[]{:S(2)}) async-start(bf16[16,16,512]{2,1,0:T(8,128)(2,1)} %spread.1), calls=%async_computation | async-start | bytes 524288 | tf_op jit(solution)/shard_map/all_to_all | solution.py:315
  7.2 0.7 reshape.21.gain_ref
  7.9 1.8 %prepare.1 = (f32[32,256]{1,0:T(8,128)S(1)}, bf16[32,512]{1,0:T(8,128)(2,1)S(1)}, f32[8,768]{1,0:T(8,128)S(1)}, bf16[512,1024]{1,0:T(8,128)(2,1)S(1)}, bf16[4,32...) custom-call(s32[4,16]{1,0:T(4,128)} %slot_hbm.1, s32[4]{0:T(128)} %shift_hbm.1, ...), custom_call_target="tpu_custom_call" | custom-call | bytes 20000000 | tf_op jit(solution)/shard_map/prepare/pallas_call | solution.py:320
  9.7 4.3 %all-to-all-done = bf16[16,16,512]{2,1,0:T(8,128)(2,1)S(1)} async-done(((bf16[16,16,512]{2,1,0:T(8,128)(2,1)}), bf16[16,16,512]{2,1,0:T(8,128)(2,1)S(1)}, u32[]{:S(2)}, u32[]{:S(2)}) %all-to-all-start) | async-done | bytes 262176 | tf_op jit(solution)/shard_map/all_to_all | solution.py:315
  14.0 0.0 copy-start
  14.0 2.5 %project.1 = bf16[16,112,128]{2,1,0:T(8,128)(2,1)S(1)} custom-call(bf16[256,512]{1,0:T(8,128)(2,1)S(1)} %bitcast.5, f32[32,256]{1,0:T(8,128)S(1)} %get-tuple-element.14.pick_ref, bf16[1,512]{1,0:T(2,128)(2,1)S(1)} %reshape.21.gain_ref, bf16[512,1024]{1,0:T(8,128)(2,1)S(1)} %get-tuple-element.15.wkv_ref, bf16[4,32,512]{2,1,0:T(8,128)(2,1)S(1)} %get-tuple-element.16.kc_ref, ...), custom_call_target="tpu_custom_call" | custom-call | tf_op jit(solution)/shard_map/project/pallas_call | solution.py:353
  16.5 27.8 %all_to_all.20.in_ref = bf16[16,112,128]{2,1,0:T(8,128)(2,1)S(1)} all-to-all(bf16[16,112,128]{2,1,0:T(8,128)(2,1)S(1)} %project.1), channel_id=1, replica_groups=mesh['group'=16,'seq_y'=4,'seq_z'=4] {'seq_y','seq_z'}, dimensions={0} | all-to-all | bytes 917504 | tf_op jit(solution)/shard_map/all_to_all | solution.py:372
  44.3 0.5 attend.1
  44.9 14.9 %all_to_all.21 = bf16[64,8,128]{2,1,0:T(8,128)(2,1)S(1)} all-to-all(bf16[64,8,128]{2,1,0:T(8,128)(2,1)S(1)} %bitcast.7), channel_id=1, replica_groups=mesh['group'=16,'seq_y'=4,'seq_z'=4] {'group','seq_z'}, dimensions={0} | all-to-all | bytes 262144 | tf_op jit(solution)/shard_map/all_to_all | solution.py:382
  59.7 0.0 copy-done
  59.7 0.8 output.1
  60.5 16.7 %all_to_all.22.in_ref = bf16[16,16,512]{2,1,0:T(8,128)(2,1)S(1)} all-to-all(bf16[16,16,512]{2,1,0:T(8,128)(2,1)S(1)} %output.1), channel_id=1, replica_groups=mesh['group'=16,'seq_y'=4,'seq_z'=4] {'seq_y','seq_z'}, dimensions={0} | all-to-all | bytes 524288 | tf_op jit(solution)/shard_map/all_to_all | solution.py:394
  77.2 0.6 gather.1
Async XLA Ops:
  1.5 12.6 %all-to-all-start = ((bf16[16,16,512]{2,1,0:T(8,128)(2,1)}), bf16[16,16,512]{2,1,0:T(8,128)(2,1)S(1)}, u32[]{:S(2)}, u32[]{:S(2)}) async-start(bf16[16,16,512]{2,1,0:T(8,128)(2,1)} %spread.1), calls=%async_computation | async-start | bytes 524288 | tf_op jit(solution)/shard_map/all_to_all | solution.py:315
  14.0 45.7 %copy-start = (bf16[256,8192]{1,0:T(8,128)(2,1)S(1)}, bf16[256,8192]{1,0:T(8,128)(2,1)}, u32[]{:S(2)}) copy-start(bf16[256,8192]{1,0:T(8,128)(2,1)} %w_ref.1) | copy-start | bytes 12582916

commit v3 on v2

--- a/solution.py
+++ b/solution.py
@@ -54,6 +54,13 @@
     return jnp.where(value >= GROUPS, value - GROUPS, value)
 
 
+def ring(value):
+    return value ^ (value >> 1)
+
+
+SEQ_ORDER = [ring(y) * 4 + ring(z) for y in range(4) for z in range(4)]
+
+
 def spread_kernel(x_hbm, out_ref, x_ref, sem):
     copy = pltpu.make_async_copy(x_hbm, x_ref, sem)
     copy.start()
@@ -72,15 +79,12 @@
     freq_hbm,
     wq_hbm,
     wkv_hbm,
-    kc_hbm,
-    vc_hbm,
     pick_in_ref,
     pick_out_ref,
     table_ref,
     wkv_ref,
-    kc_ref,
-    vc_ref,
     wq0_ref,
+    wq1_ref,
     slot_ref,
     shift_ref,
     len_ref,
@@ -91,15 +95,12 @@
         pltpu.make_async_copy(slot_hbm, slot_ref, sems.at[0]),
         pltpu.make_async_copy(shift_hbm, shift_ref, sems.at[1]),
         pltpu.make_async_copy(len_hbm, len_ref, sems.at[2]),
-        pltpu.make_async_copy(freq_hbm, freq_ref, sems.at[7]),
+        pltpu.make_async_copy(freq_hbm, freq_ref, sems.at[6]),
     ]
-    large = [
-        pltpu.make_async_copy(kc_hbm, kc_ref, sems.at[3]),
-        pltpu.make_async_copy(vc_hbm, vc_ref, sems.at[4]),
-        pltpu.make_async_copy(wkv_hbm, wkv_ref, sems.at[5]),
-    ]
-    columns = pl.ds(0, wq0_ref.shape[1])
-    large.append(pltpu.make_async_copy(wq_hbm.at[:, columns], wq0_ref, sems.at[6]))
+    large = [pltpu.make_async_copy(wkv_hbm, wkv_ref, sems.at[3])]
+    for k, part in enumerate((wq0_ref, wq1_ref)):
+        columns = pl.ds(k * part.shape[1], part.shape[1])
+        large.append(pltpu.make_async_copy(wq_hbm.at[:, columns], part, sems.at[4 + k]))
     for copy in small + large:
         copy.start()
     for copy in small:
@@ -165,21 +166,29 @@
     pick_ref,
     gain_ref,
     wkv_ref,
-    kc_ref,
-    vc_ref,
     wq0_ref,
+    wq1_ref,
     wq_hbm,
+    kc_hbm,
+    vc_hbm,
     out_ref,
-    wq1_ref,
     wq2_ref,
     wq3_ref,
     sems,
+    cache_sems,
 ):
     copies = []
-    for k, part in enumerate((wq1_ref, wq2_ref, wq3_ref)):
-        columns = pl.ds((1 + k) * part.shape[1], part.shape[1])
+    for k, part in enumerate((wq2_ref, wq3_ref)):
+        columns = pl.ds((2 + k) * part.shape[1], part.shape[1])
         copies.append(pltpu.make_async_copy(wq_hbm.at[:, columns], part, sems.at[k]))
         copies[k].start(priority=1)
+    cached = []
+    for k in range(KVH):
+        for part, cache in enumerate((kc_hbm, vc_hbm)):
+            source = cache.at[:, :, pl.ds(k * HD, HD)]
+            target = out_ref.at[pl.ds(k * REQ, REQ), pl.ds(part * LOCAL, LOCAL), :]
+            cached.append(pltpu.make_async_copy(source, target, cache_sems.at[2 * k + part]))
+            cached[-1].start()
     row8 = lax.broadcasted_iota(jnp.int32, (8, HD), 0)
     x = jnp.dot(pick_ref[...].astype(bf16), x_ref[...], preferred_element_type=f32)
     squares = jnp.sum(x * x, axis=-1, keepdims=True)
@@ -189,8 +198,8 @@
     lanes = lax.broadcasted_iota(jnp.int32, squares.shape, 1)
     squares = jnp.where(lanes < HD // 2, high, squares - high)
     for k, wq_ref in enumerate((wq0_ref, wq1_ref, wq2_ref, wq3_ref)):
-        if k >= 1:
-            copies[k - 1].wait()
+        if k >= 2:
+            copies[k - 2].wait()
         query = jnp.dot(normed, wq_ref[...], preferred_element_type=f32)
         key = jnp.dot(normed, wkv_ref[:, k * HD : (k + 1) * HD], preferred_element_type=f32)
         value = jnp.dot(
@@ -211,9 +220,9 @@
             tiles.append(jnp.where(row8 < 4, key[rows], value[rows]))
             tiles.append(squares[rows])
             at = k * REQ + r
-            out_ref[at, 0:LOCAL, :] = kc_ref[r, :, k * HD : (k + 1) * HD]
-            out_ref[at, LOCAL : 2 * LOCAL, :] = vc_ref[r, :, k * HD : (k + 1) * HD]
             out_ref[at, 2 * LOCAL : CHUNK, :] = jnp.concatenate(tiles, axis=0).astype(bf16)
+    for copy in cached:
+        copy.wait()
 
 
 def attend_kernel(table_ref, in_ref, out_ref):
@@ -273,7 +282,7 @@
     width = out_ref.shape[2]
     for k in range(SEQ):
         columns = slice(k * width, (k + 1) * width)
-        out_ref[k] = jnp.dot(
+        out_ref[SEQ_ORDER.index(k)] = jnp.dot(
             attention, w_ref[:, columns], preferred_element_type=f32
         ).astype(bf16)
 
@@ -316,26 +325,26 @@
 
     half = np.arange(HD) % (HD // 2)
     freq = jnp.asarray((rope_base ** (-2.0 * half / HD)).astype(np.float32).reshape(1, HD))
-    large = (w_query, w_keyval, key_cache, value_cache)
-    pick_in, pick_out, table, wkv, kc, vc, *split = pl.pallas_call(
+    large = (w_query, w_keyval)
+    pick_in, pick_out, table, wkv, *split = pl.pallas_call(
         prepare_kernel,
         in_specs=[anywhere()] * 3
         + [pl.BlockSpec(memory_space=pltpu.SMEM)] * 2
-        + [anywhere()] * 5,
-        out_specs=[in_vmem()] * 7,
+        + [anywhere()] * 3,
+        out_specs=[in_vmem()] * 6,
         out_shape=[
             pltpu.VMEM((8 * REQ, GROUPS * ROWS), f32),
             pltpu.VMEM((2 * ROWS, GROUPS * REQ * 8), bf16),
             pltpu.VMEM((8, 2 * HD + CONTEXT), f32),
         ]
-        + [pltpu.VMEM(array.shape, bf16) for array in (w_keyval, key_cache, value_cache)]
-        + [pltpu.VMEM((width, PER_KV * HD), bf16)],
+        + [pltpu.VMEM(w_keyval.shape, bf16)]
+        + [pltpu.VMEM((width, PER_KV * HD), bf16)] * 2,
         scratch_shapes=[
             pltpu.SMEM(mig_slot.shape, jnp.int32),
             pltpu.SMEM(mig_shift.shape, jnp.int32),
             pltpu.SMEM(ctx_len.shape, jnp.int32),
             pltpu.VMEM((1, HD), f32),
-            pltpu.SemaphoreType.DMA((8,)),
+            pltpu.SemaphoreType.DMA((7,)),
         ],
         compiler_params=params(),
         cost_estimate=pl.CostEstimate(flops=0, bytes_accessed=20_000_000, transcendentals=0),
@@ -352,11 +361,11 @@
 
     sent = pl.pallas_call(
         project_kernel,
-        in_specs=[in_vmem()] * 7 + [anywhere()],
+        in_specs=[in_vmem()] * 6 + [anywhere()] * 3,
         out_specs=in_vmem(),
         out_shape=jax.ShapeDtypeStruct((SEQ, CHUNK, HD), bf16),
-        scratch_shapes=[pltpu.VMEM((width, PER_KV * HD), bf16)] * 3
-        + [pltpu.SemaphoreType.DMA((3,))],
+        scratch_shapes=[pltpu.VMEM((width, PER_KV * HD), bf16)] * 2
+        + [pltpu.SemaphoreType.DMA((2,)), pltpu.SemaphoreType.DMA((2 * KVH,))],
         compiler_params=params(),
         name="project",
     )(
@@ -364,10 +373,10 @@
         placed(pick_in),
         norm_gain.reshape(1, width),
         placed(wkv),
-        placed(kc),
-        placed(vc),
         *[placed(part) for part in split],
         left(w_query),
+        left(key_cache),
+        left(value_cache),
     )
     received = lax.all_to_all(sent, seq, 0, 0, tiled=True)
 
@@ -391,7 +400,9 @@
         compiler_params=params(),
         name="output",
     )(placed(pick_out), attention, placed(w_out))
-    shares = lax.all_to_all(shares, seq, 0, 0, tiled=True)
+    shares = lax.all_to_all(
+        shares, seq, 0, 0, tiled=True, axis_index_groups=[SEQ_ORDER]
+    )
     return pl.pallas_call(
         gather_kernel,
         in_specs=[in_vmem()],

time: 78.9 us -> 77.5 us (0.982)
  transfers between devices with their start and end apart: 1 -> 1, of which waited for: 1 -> 1; matrix products, arithmetic and copies ran while one was open for 1% -> 1% of each run, Pallas kernels for 2% -> 3%
where the time goes in v3:
time: 77.5 us; the launch traced here: 77 us
  blocking collectives  58.7 us (76%)
  Pallas kernels  7.62 us (10%)
  starting transfers between devices  5.79 us (7%)
  waiting for transfers between devices  4.16 us (5%)
    all_to_all x1, blocking collectives, body(): received = lax.all_to_all(sent, seq, 0, 0, tiled=True)  27.8 us
    all_to_all x1, blocking collectives, body(): lax.all_to_all(shares, seq, 0, 0, tiled=True, axis_index_groups=[SEQ_ORDER])  16.1 us
    all_to_all x1, blocking collectives, body(): lax.all_to_all(attention.reshape(GROUPS * 4, 8, HD), ('group', 'seq_z'),...  14.9 us
    all_to_all x1, starting transfers between devices, body(): lax.all_to_all(x, 'group', 0, 0, tiled=True).reshape(GROUPS * ROWS, width)  5.79 us
    all_to_all x1, waiting for transfers between devices, body(): lax.all_to_all(x, 'group', 0, 0, tiled=True).reshape(GROUPS * ROWS, width)  4.16 us
    pallas_call x1, Pallas kernels, body(): pl.pallas_call(project_kernel, in_specs=[in_vmem()] * 6 + [anywhere()] *...  2.31 us
    pallas_call x1, Pallas kernels, body(): pl.pallas_call(prepare_kernel, in_specs=[anywhere()] * 3 + [pl.BlockSpec(...  1.94 us
  transfers between devices with their start and end apart: 1, of which 1 were waited for; matrix products, arithmetic and copies ran while one was open for 1% of the time, Pallas kernels for 3%

profile of v3, /device:TPU:32, one launch (start us, length us, event | category | flops | bytes accessed | tf_op | source)
XLA Modules:
  0.0 77.0 jit_solution(16829073041968080988)
XLA Ops:
  0.0 1.4 %spread.1 = bf16[16,16,512]{2,1,0:T(8,128)(2,1)} custom-call(bf16[4,4,512]{2,1,0:T(4,128)(2,1)} %x_hbm.1), custom_call_target="tpu_custom_call" | custom-call | tf_op jit(solution)/shard_map/spread/pallas_call | solution.py:315
  1.5 5.8 %all-to-all-start = ((bf16[16,16,512]{2,1,0:T(8,128)(2,1)}), bf16[16,16,512]{2,1,0:T(8,128)(2,1)S(1)}, u32[]{:S(2)}, u32[]{:S(2)}) async-start(bf16[16,16,512]{2,1,0:T(8,128)(2,1)} %spread.1), calls=%async_computation | async-start | bytes 524288 | tf_op jit(solution)/shard_map/all_to_all | solution.py:324
  7.2 0.7 reshape.21.gain_ref
  7.9 1.9 %prepare.1 = (f32[32,256]{1,0:T(8,128)S(1)}, bf16[32,512]{1,0:T(8,128)(2,1)S(1)}, f32[8,768]{1,0:T(8,128)S(1)}, bf16[512,1024]{1,0:T(8,128)(2,1)S(1)}, bf16[512,...) custom-call(s32[4,16]{1,0:T(4,128)} %slot_hbm.1, s32[4]{0:T(128)} %shift_hbm.1, s32[4]{0:T(128)} %len_hbm.1, ...), custom_call_target="tpu_custom_call" | custom-call | bytes 20000000 | tf_op jit(solution)/shard_map/prepare/pallas_call | solution.py:329
  9.9 4.2 %all-to-all-done = bf16[16,16,512]{2,1,0:T(8,128)(2,1)S(1)} async-done(((bf16[16,16,512]{2,1,0:T(8,128)(2,1)}), bf16[16,16,512]{2,1,0:T(8,128)(2,1)S(1)}, u32[]{:S(2)}, u32[]{:S(2)}) %all-to-all-start) | async-done | bytes 262176 | tf_op jit(solution)/shard_map/all_to_all | solution.py:324
  14.0 0.0 copy-start
  14.0 2.3 %project.1 = bf16[16,112,128]{2,1,0:T(8,128)(2,1)S(1)} custom-call(bf16[256,512]{1,0:T(8,128)(2,1)S(1)} %bitcast.5, f32[32,256]{1,0:T(8,128)S(1)} %get-tuple-element.13.pick_ref, bf16[1,512]{1,0:T(2,128)(2,1)S(1)} %reshape.21.gain_ref, bf16[512,1024]{1,0:T(8,128)(2,1)S(1)} %get-tuple-element.14.wkv_ref, bf16[512,1024]{1,0:T(8,128)(2,1)S(1)} %get-tuple-element.15.wq0_ref, ...), custom_call_target="tpu_custom_call" | custom-call | tf_op jit(solution)/shard_map/project/pallas_call | solution.py:362
  16.3 27.8 %all_to_all.20.in_ref = bf16[16,112,128]{2,1,0:T(8,128)(2,1)S(1)} all-to-all(bf16[16,112,128]{2,1,0:T(8,128)(2,1)S(1)} %project.1), channel_id=1, replica_groups=mesh['group'=16,'seq_y'=4,'seq_z'=4] {'seq_y','seq_z'}, dimensions={0} | all-to-all | bytes 917504 | tf_op jit(solution)/shard_map/all_to_all | solution.py:381
  44.2 0.5 attend.1
  44.7 14.9 %all_to_all.21 = bf16[64,8,128]{2,1,0:T(8,128)(2,1)S(1)} all-to-all(bf16[64,8,128]{2,1,0:T(8,128)(2,1)S(1)} %bitcast.7), channel_id=1, replica_groups=mesh['group'=16,'seq_y'=4,'seq_z'=4] {'group','seq_z'}, dimensions={0} | all-to-all | bytes 262144 | tf_op jit(solution)/shard_map/all_to_all | solution.py:391
  59.6 0.0 copy-done
  59.6 0.8 output.1
  60.3 16.1 %all_to_all.22.in_ref = bf16[16,16,512]{2,1,0:T(8,128)(2,1)S(1)} all-to-all(bf16[16,16,512]{2,1,0:T(8,128)(2,1)S(1)} %output.1), channel_id=1, replica_groups={{0,1,3,2,4,5,7,6,12,13,15,14,8,9,11,10},{16,17,19,18,20,21,23,22,28,29,..., dimensions={0} | all-to-all | bytes 524288 | tf_op jit(solution)/shard_map/all_to_all | solution.py:403
  76.4 0.6 gather.1
Async XLA Ops:
  1.5 12.6 %all-to-all-start = ((bf16[16,16,512]{2,1,0:T(8,128)(2,1)}), bf16[16,16,512]{2,1,0:T(8,128)(2,1)S(1)}, u32[]{:S(2)}, u32[]{:S(2)}) async-start(bf16[16,16,512]{2,1,0:T(8,128)(2,1)} %spread.1), calls=%async_computation | async-start | bytes 524288 | tf_op jit(solution)/shard_map/all_to_all | solution.py:324
  14.0 45.5 %copy-start = (bf16[256,8192]{1,0:T(8,128)(2,1)S(1)}, bf16[256,8192]{1,0:T(8,128)(2,1)}, u32[]{:S(2)}) copy-start(bf16[256,8192]{1,0:T(8,128)(2,1)} %w_ref.1) | copy-start | bytes 12582916

commit v4 on v3

--- a/solution.py
+++ b/solution.py
@@ -54,11 +54,7 @@
     return jnp.where(value >= GROUPS, value - GROUPS, value)
 
 
-def ring(value):
-    return value ^ (value >> 1)
-
-
-SEQ_ORDER = [ring(y) * 4 + ring(z) for y in range(4) for z in range(4)]
+SEQ_ORDER = [4 * y + (z if y % 2 == 0 else 3 - z) for y in range(4) for z in range(4)]
 
 
 def spread_kernel(x_hbm, out_ref, x_ref, sem):

time: 77.5 us -> 77.1 us (level)
  no operation moved by 1% of the time
where the time goes in v4:
time: 77.1 us; the launch traced here: 76.7 us
  blocking collectives  58.4 us (76%)
  Pallas kernels  7.62 us (10%)
  starting transfers between devices  5.79 us (8%)
  waiting for transfers between devices  4.16 us (5%)
    all_to_all x1, blocking collectives, body(): received = lax.all_to_all(sent, seq, 0, 0, tiled=True)  27.8 us
    all_to_all x1, blocking collectives, body(): lax.all_to_all(shares, seq, 0, 0, tiled=True, axis_index_groups=[SEQ_ORDER])  15.7 us
    all_to_all x1, blocking collectives, body(): lax.all_to_all(attention.reshape(GROUPS * 4, 8, HD), ('group', 'seq_z'),...  14.9 us
    all_to_all x1, starting transfers between devices, body(): lax.all_to_all(x, 'group', 0, 0, tiled=True).reshape(GROUPS * ROWS, width)  5.79 us
    all_to_all x1, waiting for transfers between devices, body(): lax.all_to_all(x, 'group', 0, 0, tiled=True).reshape(GROUPS * ROWS, width)  4.16 us
    pallas_call x1, Pallas kernels, body(): pl.pallas_call(project_kernel, in_specs=[in_vmem()] * 6 + [anywhere()] *...  2.31 us
    pallas_call x1, Pallas kernels, body(): pl.pallas_call(prepare_kernel, in_specs=[anywhere()] * 3 + [pl.BlockSpec(...  1.94 us
  transfers between devices with their start and end apart: 1, of which 1 were waited for; matrix products, arithmetic and copies ran while one was open for 1% of the time, Pallas kernels for 3%

profile of v4, /device:TPU:32, one launch (start us, length us, event | category | flops | bytes accessed | tf_op | source)
XLA Modules:
  0.0 76.7 jit_solution(16502509427138769568)
XLA Ops:
  0.0 1.4 %spread.1 = bf16[16,16,512]{2,1,0:T(8,128)(2,1)} custom-call(bf16[4,4,512]{2,1,0:T(4,128)(2,1)} %x_hbm.1), custom_call_target="tpu_custom_call" | custom-call | tf_op jit(solution)/shard_map/spread/pallas_call | solution.py:311
  1.5 5.8 %all-to-all-start = ((bf16[16,16,512]{2,1,0:T(8,128)(2,1)}), bf16[16,16,512]{2,1,0:T(8,128)(2,1)S(1)}, u32[]{:S(2)}, u32[]{:S(2)}) async-start(bf16[16,16,512]{2,1,0:T(8,128)(2,1)} %spread.1), calls=%async_computation | async-start | bytes 524288 | tf_op jit(solution)/shard_map/all_to_all | solution.py:320
  7.2 0.7 reshape.21.gain_ref
  7.9 1.9 %prepare.1 = (f32[32,256]{1,0:T(8,128)S(1)}, bf16[32,512]{1,0:T(8,128)(2,1)S(1)}, f32[8,768]{1,0:T(8,128)S(1)}, bf16[512,1024]{1,0:T(8,128)(2,1)S(1)}, bf16[512,...) custom-call(s32[4,16]{1,0:T(4,128)} %slot_hbm.1, s32[4]{0:T(128)} %shift_hbm.1, s32[4]{0:T(128)} %len_hbm.1, ...), custom_call_target="tpu_custom_call" | custom-call | bytes 20000000 | tf_op jit(solution)/shard_map/prepare/pallas_call | solution.py:325
  9.9 4.2 %all-to-all-done = bf16[16,16,512]{2,1,0:T(8,128)(2,1)S(1)} async-done(((bf16[16,16,512]{2,1,0:T(8,128)(2,1)}), bf16[16,16,512]{2,1,0:T(8,128)(2,1)S(1)}, u32[]{:S(2)}, u32[]{:S(2)}) %all-to-all-start) | async-done | bytes 262176 | tf_op jit(solution)/shard_map/all_to_all | solution.py:320
  14.0 0.0 copy-start
  14.0 2.3 %project.1 = bf16[16,112,128]{2,1,0:T(8,128)(2,1)S(1)} custom-call(bf16[256,512]{1,0:T(8,128)(2,1)S(1)} %bitcast.5, f32[32,256]{1,0:T(8,128)S(1)} %get-tuple-element.13.pick_ref, bf16[1,512]{1,0:T(2,128)(2,1)S(1)} %reshape.21.gain_ref, bf16[512,1024]{1,0:T(8,128)(2,1)S(1)} %get-tuple-element.14.wkv_ref, bf16[512,1024]{1,0:T(8,128)(2,1)S(1)} %get-tuple-element.15.wq0_ref, ...), custom_call_target="tpu_custom_call" | custom-call | tf_op jit(solution)/shard_map/project/pallas_call | solution.py:358
  16.3 27.8 %all_to_all.20.in_ref = bf16[16,112,128]{2,1,0:T(8,128)(2,1)S(1)} all-to-all(bf16[16,112,128]{2,1,0:T(8,128)(2,1)S(1)} %project.1), channel_id=1, replica_groups=mesh['group'=16,'seq_y'=4,'seq_z'=4] {'seq_y','seq_z'}, dimensions={0} | all-to-all | bytes 917504 | tf_op jit(solution)/shard_map/all_to_all | solution.py:377
  44.2 0.5 attend.1
  44.7 14.9 %all_to_all.21 = bf16[64,8,128]{2,1,0:T(8,128)(2,1)S(1)} all-to-all(bf16[64,8,128]{2,1,0:T(8,128)(2,1)S(1)} %bitcast.7), channel_id=1, replica_groups=mesh['group'=16,'seq_y'=4,'seq_z'=4] {'group','seq_z'}, dimensions={0} | all-to-all | bytes 262144 | tf_op jit(solution)/shard_map/all_to_all | solution.py:387
  59.6 0.0 copy-done
  59.6 0.8 output.1
  60.3 15.7 %all_to_all.22.in_ref = bf16[16,16,512]{2,1,0:T(8,128)(2,1)S(1)} all-to-all(bf16[16,16,512]{2,1,0:T(8,128)(2,1)S(1)} %output.1), channel_id=1, replica_groups={{0,1,2,3,7,6,5,4,8,9,10,11,15,14,13,12},{16,17,18,19,23,22,21,20,24,25,..., dimensions={0} | all-to-all | bytes 524288 | tf_op jit(solution)/shard_map/all_to_all | solution.py:399
  76.0 0.6 gather.1
Async XLA Ops:
  1.5 12.6 %all-to-all-start = ((bf16[16,16,512]{2,1,0:T(8,128)(2,1)}), bf16[16,16,512]{2,1,0:T(8,128)(2,1)S(1)}, u32[]{:S(2)}, u32[]{:S(2)}) async-start(bf16[16,16,512]{2,1,0:T(8,128)(2,1)} %spread.1), calls=%async_computation | async-start | bytes 524288 | tf_op jit(solution)/shard_map/all_to_all | solution.py:320
  14.0 45.5 %copy-start = (bf16[256,8192]{1,0:T(8,128)(2,1)S(1)}, bf16[256,8192]{1,0:T(8,128)(2,1)}, u32[]{:S(2)}) copy-start(bf16[256,8192]{1,0:T(8,128)(2,1)} %w_ref.1) | copy-start | bytes 12582916

commit v5 on v4

--- a/solution.py
+++ b/solution.py
@@ -15,6 +15,7 @@
 REQ = 4
 GROUPS = 16
 SEQ = 16
+CHIPS = GROUPS // 2
 PER_KV = H // KVH
 LOCAL = 32
 CONTEXT = SEQ * LOCAL
@@ -136,7 +137,8 @@
                 source_slot = slot_ref[back, source]
                 at_group = jnp.where(came, source, at_group)
                 at_slot = jnp.where(came, source_slot, at_slot)
-            column = (at_group * REQ + at_slot) * 8 + s
+            column = ((at_group >> 1) * REQ + at_slot) * 8 + s
+            column = column + ((at_group ^ group) & 1) * (CHIPS * REQ * 8)
             target = jnp.where((row & (ROWS - 1)) == s * REQ + r, column, target)
     target = target + jnp.where(row >= ROWS, 4, 0)
     for part in range(GROUPS * REQ * 8 // HD):
@@ -268,12 +270,14 @@
     )
     attention = (summed / count).astype(bf16)
     rows = attention.shape[0]
-    for g in range(GROUPS):
+    for g in range(CHIPS):
         out_ref[g * rows : (g + 1) * rows, :] = attention
 
 
-def output_kernel(pick_ref, in_ref, w_ref, out_ref):
-    picked = jnp.dot(pick_ref[...], in_ref[...], preferred_element_type=f32)
+def output_kernel(pick_ref, in_ref, other_ref, w_ref, out_ref):
+    half = CHIPS * REQ * 8
+    picked = jnp.dot(pick_ref[:, :half], in_ref[...], preferred_element_type=f32)
+    picked = picked + jnp.dot(pick_ref[:, half:], other_ref[...], preferred_element_type=f32)
     attention = jnp.concatenate([picked[0:ROWS], picked[ROWS : 2 * ROWS]], axis=1).astype(bf16)
     width = out_ref.shape[2]
     for k in range(SEQ):
@@ -305,7 +309,7 @@
 ):
     width = step_inputs.shape[2]
     seq = ("seq_y", "seq_z")
-    group = lax.axis_index("group").astype(jnp.int32).reshape(1)
+    group = lax.axis_index(("chip", "core")).astype(jnp.int32).reshape(1)
     own = lax.axis_index("seq_z").astype(jnp.int32).reshape(1)
 
     x = pl.pallas_call(
@@ -317,7 +321,7 @@
         compiler_params=params(),
         name="spread",
     )(left(step_inputs))
-    x = lax.all_to_all(x, "group", 0, 0, tiled=True).reshape(GROUPS * ROWS, width)
+    x = lax.all_to_all(x, ("chip", "core"), 0, 0, tiled=True).reshape(GROUPS * ROWS, width)
 
     half = np.arange(HD) % (HD // 2)
     freq = jnp.asarray((rope_base ** (-2.0 * half / HD)).astype(np.float32).reshape(1, HD))
@@ -380,22 +384,23 @@
         attend_kernel,
         in_specs=[in_vmem()] * 2,
         out_specs=in_vmem(),
-        out_shape=jax.ShapeDtypeStruct((GROUPS * PER_KV * STEPS, HD), bf16),
+        out_shape=jax.ShapeDtypeStruct((CHIPS * PER_KV * STEPS, HD), bf16),
         compiler_params=params(),
         name="attend",
     )(placed(table), received)
     attention = lax.all_to_all(
-        attention.reshape(GROUPS * 4, 8, HD), ("group", "seq_z"), 0, 0, tiled=True
-    ).reshape(GROUPS * 4 * 8, HD)
+        attention.reshape(CHIPS * 4, 8, HD), ("chip", "seq_z"), 0, 0, tiled=True
+    ).reshape(CHIPS * 4 * 8, HD)
+    other = lax.ppermute(attention, "core", [(0, 1), (1, 0)])
 
     shares = pl.pallas_call(
         output_kernel,
-        in_specs=[in_vmem()] * 3,
+        in_specs=[in_vmem()] * 4,
         out_specs=in_vmem(),
         out_shape=jax.ShapeDtypeStruct((SEQ, ROWS, width), bf16),
         compiler_params=params(),
         name="output",
-    )(placed(pick_out), attention, placed(w_out))
+    )(placed(pick_out), attention, other, placed(w_out))
     shares = lax.all_to_all(
         shares, seq, 0, 0, tiled=True, axis_index_groups=[SEQ_ORDER]
     )
@@ -410,20 +415,21 @@
 
 
 def solution(mesh):
-    split = Mesh(mesh.devices.reshape(GROUPS, 4, 4), ("group", "seq_y", "seq_z"))
+    split = Mesh(mesh.devices.reshape(GROUPS // 2, 2, 4, 4), ("chip", "core", "seq_y", "seq_z"))
     seq = ("seq_y", "seq_z")
+    group = ("chip", "core")
     specs = (
-        P(None, "group", seq),
+        P(None, group, seq),
         P(seq),
         P(seq, None),
         P(seq, None),
         P(seq, None),
-        P("group", seq, None),
-        P("group", seq, None),
-        P("group"),
+        P(group, seq, None),
+        P(group, seq, None),
+        P(group),
         P(),
         P(),
     )
     return jax.shard_map(
-        body, mesh=split, in_specs=specs, out_specs=P(None, "group", seq), check_vma=False
-    )
+        body, mesh=split, in_specs=specs, out_specs=P(None, group, seq), check_vma=False
+    )

time: 77.1 us -> 76.8 us (level)
  blocking collectives: 58.4 us -> 56.9 us
  waiting for transfers between devices: 4.16 us -> 5.41 us
    all_to_all x1, blocking collectives: 14.9 us -> 12.9 us  [body(): lax.all_to_all(attention.reshape(CHIPS * 4, 8, HD), ('chip', 'seq_z'), 0,...]
    ppermute x0 -> x1, waiting for transfers between devices: none -> 1.25 us  [body(): other = lax.ppermute(attention, 'core', [(0, 1), (1, 0)])]
  transfers between devices with their start and end apart: 1 -> 2, of which waited for: 1 -> 2; matrix products, arithmetic and copies ran while one was open for 1% -> 1% of each run, Pallas kernels for 3% -> 3%
where the time goes in v5:
time: 76.8 us; the launch traced here: 76.4 us
  blocking collectives  56.9 us (74%)
  Pallas kernels  7.62 us (10%)
  starting transfers between devices  5.79 us (8%)
  waiting for transfers between devices  5.41 us (7%)
    all_to_all x1, blocking collectives, body(): received = lax.all_to_all(sent, seq, 0, 0, tiled=True)  27.8 us
    all_to_all x1, blocking collectives, body(): lax.all_to_all(shares, seq, 0, 0, tiled=True, axis_index_groups=[SEQ_ORDER])  16.1 us
    all_to_all x1, blocking collectives, body(): lax.all_to_all(attention.reshape(CHIPS * 4, 8, HD), ('chip', 'seq_z'), 0,...  12.9 us
    all_to_all x1, starting transfers between devices, body(): lax.all_to_all(x, ('chip', 'core'), 0, 0, tiled=True)  5.79 us
    all_to_all x1, waiting for transfers between devices, body(): lax.all_to_all(x, ('chip', 'core'), 0, 0, tiled=True)  4.16 us
    pallas_call x1, Pallas kernels, body(): pl.pallas_call(project_kernel, in_specs=[in_vmem()] * 6 + [anywhere()] *...  2.31 us
    pallas_call x1, Pallas kernels, body(): pl.pallas_call(prepare_kernel, in_specs=[anywhere()] * 3 + [pl.BlockSpec(...  1.94 us
  transfers between devices with their start and end apart: 2, of which 2 were waited for; matrix products, arithmetic and copies ran while one was open for 1% of the time, Pallas kernels for 3%

profile of v5, /device:TPU:32, one launch (start us, length us, event | category | flops | bytes accessed | tf_op | source)
XLA Modules:
  0.0 76.4 jit_solution(14989005585624736709)
XLA Ops:
  0.0 1.4 %spread.1 = bf16[16,16,512]{2,1,0:T(8,128)(2,1)} custom-call(bf16[4,4,512]{2,1,0:T(4,128)(2,1)} %x_hbm.1), custom_call_target="tpu_custom_call" | custom-call | tf_op jit(solution)/shard_map/spread/pallas_call | solution.py:315
  1.5 5.8 %all-to-all-start = ((bf16[16,16,512]{2,1,0:T(8,128)(2,1)}), bf16[16,16,512]{2,1,0:T(8,128)(2,1)S(1)}, u32[]{:S(2)}, u32[]{:S(2)}) async-start(bf16[16,16,512]{2,1,0:T(8,128)(2,1)} %spread.1), calls=%async_computation | async-start | bytes 524288 | tf_op jit(solution)/shard_map/all_to_all | solution.py:324
  7.2 0.7 reshape.21.gain_ref
  7.9 1.9 %prepare.1 = (f32[32,256]{1,0:T(8,128)S(1)}, bf16[32,512]{1,0:T(8,128)(2,1)S(1)}, f32[8,768]{1,0:T(8,128)S(1)}, bf16[512,1024]{1,0:T(8,128)(2,1)S(1)}, bf16[512,...) custom-call(s32[4,16]{1,0:T(4,128)} %slot_hbm.1, s32[4]{0:T(128)} %shift_hbm.1, s32[4]{0:T(128)} %len_hbm.1, ...), custom_call_target="tpu_custom_call" | custom-call | bytes 20000000 | tf_op jit(solution)/shard_map/prepare/pallas_call | solution.py:329
  9.9 4.2 %all-to-all-done = bf16[16,16,512]{2,1,0:T(8,128)(2,1)S(1)} async-done(((bf16[16,16,512]{2,1,0:T(8,128)(2,1)}), bf16[16,16,512]{2,1,0:T(8,128)(2,1)S(1)}, u32[]{:S(2)}, u32[]{:S(2)}) %all-to-all-start) | async-done | bytes 262176 | tf_op jit(solution)/shard_map/all_to_all | solution.py:324
  14.0 0.0 copy-start
  14.0 2.3 %project.1 = bf16[16,112,128]{2,1,0:T(8,128)(2,1)S(1)} custom-call(bf16[256,512]{1,0:T(8,128)(2,1)S(1)} %bitcast.5, f32[32,256]{1,0:T(8,128)S(1)} %get-tuple-element.13.pick_ref, bf16[1,512]{1,0:T(2,128)(2,1)S(1)} %reshape.21.gain_ref, bf16[512,1024]{1,0:T(8,128)(2,1)S(1)} %get-tuple-element.14.wkv_ref, bf16[512,1024]{1,0:T(8,128)(2,1)S(1)} %get-tuple-element.15.wq0_ref, ...), custom_call_target="tpu_custom_call" | custom-call | tf_op jit(solution)/shard_map/project/pallas_call | solution.py:362
  16.3 27.8 %all_to_all.20.in_ref = bf16[16,112,128]{2,1,0:T(8,128)(2,1)S(1)} all-to-all(bf16[16,112,128]{2,1,0:T(8,128)(2,1)S(1)} %project.1), channel_id=1, replica_groups=mesh['chip'=8,'core'=2,'seq_y'=4,'seq_z'=4] {'seq_y','seq_z'}, dimensions={0} | all-to-all | bytes 917504 | tf_op jit(solution)/shard_map/all_to_all | solution.py:381
  44.1 0.5 attend.1
  44.7 12.9 %all_to_all.21 = bf16[32,8,128]{2,1,0:T(8,128)(2,1)S(1)} all-to-all(bf16[32,8,128]{2,1,0:T(8,128)(2,1)S(1)} %bitcast.8), channel_id=1, replica_groups=mesh['chip'=8,'core'=2,'seq_y'=4,'seq_z'=4] {'chip','seq_z'}, dimensions={0} | all-to-all | bytes 131072 | tf_op jit(solution)/shard_map/all_to_all | solution.py:391
  57.6 0.0 collective-permute-start
  57.6 1.3 %collective-permute-done.other_ref = bf16[256,128]{1,0:T(8,128)(2,1)S(1)} collective-permute-done((bf16[256,128]{1,0:T(8,128)(2,1)S(1)}, bf16[256,128]{1,0:T(8,128)(2,1)S(1)}, u32[]{:S(2)}, u32[]{:S(2)}) %collective-permute-start) | collective-permute-done | bytes 65568 | tf_op jit(solution)/shard_map/ppermute | solution.py:394
  58.8 0.0 copy-done
  58.8 0.8 output.1
  59.6 16.1 %all_to_all.22.in_ref = bf16[16,16,512]{2,1,0:T(8,128)(2,1)S(1)} all-to-all(bf16[16,16,512]{2,1,0:T(8,128)(2,1)S(1)} %output.1), channel_id=1, replica_groups={{0,1,2,3,7,6,5,4,8,9,10,11,15,14,13,12},{16,17,18,19,23,22,21,20,24,25,..., dimensions={0} | all-to-all | bytes 524288 | tf_op jit(solution)/shard_map/all_to_all | solution.py:404
  75.8 0.6 gather.1
Async XLA Ops:
  1.5 12.6 %all-to-all-start = ((bf16[16,16,512]{2,1,0:T(8,128)(2,1)}), bf16[16,16,512]{2,1,0:T(8,128)(2,1)S(1)}, u32[]{:S(2)}, u32[]{:S(2)}) async-start(bf16[16,16,512]{2,1,0:T(8,128)(2,1)} %spread.1), calls=%async_computation | async-start | bytes 524288 | tf_op jit(solution)/shard_map/all_to_all | solution.py:324
  14.0 44.8 %copy-start = (bf16[256,8192]{1,0:T(8,128)(2,1)S(1)}, bf16[256,8192]{1,0:T(8,128)(2,1)}, u32[]{:S(2)}) copy-start(bf16[256,8192]{1,0:T(8,128)(2,1)} %w_ref.1) | copy-start | bytes 12582916
  57.6 1.3 %collective-permute-start = (bf16[256,128]{1,0:T(8,128)(2,1)S(1)}, bf16[256,128]{1,0:T(8,128)(2,1)S(1)}, u32[]{:S(2)}, u32[]{:S(2)}) collective-permute-start(bf16[256,128]{1,0:T(8,128)(2,1)S(1)} %bitcast.6), channel_id=1, source_target_pairs={{0,16},{16,0},{1,17},{17,1},{2,18},{18,2},{3,19},{19,3},{4,20},{20... | collective-permute-start | bytes 196616 | tf_op jit(solution)/shard_map/ppermute | solution.py:394

commit v6 on v5

--- a/solution.py
+++ b/solution.py
@@ -179,7 +179,7 @@
     for k, part in enumerate((wq2_ref, wq3_ref)):
         columns = pl.ds((2 + k) * part.shape[1], part.shape[1])
         copies.append(pltpu.make_async_copy(wq_hbm.at[:, columns], part, sems.at[k]))
-        copies[k].start(priority=1)
+        copies[k].start()
     cached = []
     for k in range(KVH):
         for part, cache in enumerate((kc_hbm, vc_hbm)):

time: 76.8 us -> 76.7 us (level)
  no operation moved by 1% of the time
where the time goes in v6:
time: 76.7 us; the launch traced here: 76.2 us
  blocking collectives  56.8 us (74%)
  Pallas kernels  7.48 us (10%)
  starting transfers between devices  5.79 us (8%)
  waiting for transfers between devices  5.41 us (7%)
    all_to_all x1, blocking collectives, body(): received = lax.all_to_all(sent, seq, 0, 0, tiled=True)  27.8 us
    all_to_all x1, blocking collectives, body(): lax.all_to_all(shares, seq, 0, 0, tiled=True, axis_index_groups=[SEQ_ORDER])  16 us
    all_to_all x1, blocking collectives, body(): lax.all_to_all(attention.reshape(CHIPS * 4, 8, HD), ('chip', 'seq_z'), 0,...  13 us
    all_to_all x1, starting transfers between devices, body(): lax.all_to_all(x, ('chip', 'core'), 0, 0, tiled=True)  5.79 us
    all_to_all x1, waiting for transfers between devices, body(): lax.all_to_all(x, ('chip', 'core'), 0, 0, tiled=True)  4.16 us
    pallas_call x1, Pallas kernels, body(): pl.pallas_call(project_kernel, in_specs=[in_vmem()] * 6 + [anywhere()] *...  2.17 us
    pallas_call x1, Pallas kernels, body(): pl.pallas_call(prepare_kernel, in_specs=[anywhere()] * 3 + [pl.BlockSpec(...  1.94 us
  transfers between devices with their start and end apart: 2, of which 2 were waited for; matrix products, arithmetic and copies ran while one was open for 1% of the time, Pallas kernels for 3%

profile of v6, /device:TPU:32, one launch (start us, length us, event | category | flops | bytes accessed | tf_op | source)
XLA Modules:
  0.0 76.2 jit_solution(4330977951945979883)
XLA Ops:
  0.0 1.4 %spread.1 = bf16[16,16,512]{2,1,0:T(8,128)(2,1)} custom-call(bf16[4,4,512]{2,1,0:T(4,128)(2,1)} %x_hbm.1), custom_call_target="tpu_custom_call" | custom-call | tf_op jit(solution)/shard_map/spread/pallas_call | solution.py:315
  1.5 5.8 %all-to-all-start = ((bf16[16,16,512]{2,1,0:T(8,128)(2,1)}), bf16[16,16,512]{2,1,0:T(8,128)(2,1)S(1)}, u32[]{:S(2)}, u32[]{:S(2)}) async-start(bf16[16,16,512]{2,1,0:T(8,128)(2,1)} %spread.1), calls=%async_computation | async-start | bytes 524288 | tf_op jit(solution)/shard_map/all_to_all | solution.py:324
  7.2 0.7 reshape.21.gain_ref
  7.9 1.9 %prepare.1 = (f32[32,256]{1,0:T(8,128)S(1)}, bf16[32,512]{1,0:T(8,128)(2,1)S(1)}, f32[8,768]{1,0:T(8,128)S(1)}, bf16[512,1024]{1,0:T(8,128)(2,1)S(1)}, bf16[512,...) custom-call(s32[4,16]{1,0:T(4,128)} %slot_hbm.1, s32[4]{0:T(128)} %shift_hbm.1, s32[4]{0:T(128)} %len_hbm.1, ...), custom_call_target="tpu_custom_call" | custom-call | bytes 20000000 | tf_op jit(solution)/shard_map/prepare/pallas_call | solution.py:329
  9.9 4.2 %all-to-all-done = bf16[16,16,512]{2,1,0:T(8,128)(2,1)S(1)} async-done(((bf16[16,16,512]{2,1,0:T(8,128)(2,1)}), bf16[16,16,512]{2,1,0:T(8,128)(2,1)S(1)}, u32[]{:S(2)}, u32[]{:S(2)}) %all-to-all-start) | async-done | bytes 262176 | tf_op jit(solution)/shard_map/all_to_all | solution.py:324
  14.0 0.0 copy-start
  14.0 2.2 %project.1 = bf16[16,112,128]{2,1,0:T(8,128)(2,1)S(1)} custom-call(bf16[256,512]{1,0:T(8,128)(2,1)S(1)} %bitcast.5, f32[32,256]{1,0:T(8,128)S(1)} %get-tuple-element.13.pick_ref, bf16[1,512]{1,0:T(2,128)(2,1)S(1)} %reshape.21.gain_ref, bf16[512,1024]{1,0:T(8,128)(2,1)S(1)} %get-tuple-element.14.wkv_ref, bf16[512,1024]{1,0:T(8,128)(2,1)S(1)} %get-tuple-element.15.wq0_ref, ...), custom_call_target="tpu_custom_call" | custom-call | tf_op jit(solution)/shard_map/project/pallas_call | solution.py:362
  16.2 27.8 %all_to_all.20.in_ref = bf16[16,112,128]{2,1,0:T(8,128)(2,1)S(1)} all-to-all(bf16[16,112,128]{2,1,0:T(8,128)(2,1)S(1)} %project.1), channel_id=1, replica_groups=mesh['chip'=8,'core'=2,'seq_y'=4,'seq_z'=4] {'seq_y','seq_z'}, dimensions={0} | all-to-all | bytes 917504 | tf_op jit(solution)/shard_map/all_to_all | solution.py:381
  44.0 0.5 attend.1
  44.6 13.0 %all_to_all.21 = bf16[32,8,128]{2,1,0:T(8,128)(2,1)S(1)} all-to-all(bf16[32,8,128]{2,1,0:T(8,128)(2,1)S(1)} %bitcast.8), channel_id=1, replica_groups=mesh['chip'=8,'core'=2,'seq_y'=4,'seq_z'=4] {'chip','seq_z'}, dimensions={0} | all-to-all | bytes 131072 | tf_op jit(solution)/shard_map/all_to_all | solution.py:391
  57.5 0.0 collective-permute-start
  57.5 1.3 %collective-permute-done.other_ref = bf16[256,128]{1,0:T(8,128)(2,1)S(1)} collective-permute-done((bf16[256,128]{1,0:T(8,128)(2,1)S(1)}, bf16[256,128]{1,0:T(8,128)(2,1)S(1)}, u32[]{:S(2)}, u32[]{:S(2)}) %collective-permute-start) | collective-permute-done | bytes 65568 | tf_op jit(solution)/shard_map/ppermute | solution.py:394
  58.8 0.0 copy-done
  58.8 0.8 output.1
  59.5 16.0 %all_to_all.22.in_ref = bf16[16,16,512]{2,1,0:T(8,128)(2,1)S(1)} all-to-all(bf16[16,16,512]{2,1,0:T(8,128)(2,1)S(1)} %output.1), channel_id=1, replica_groups={{0,1,2,3,7,6,5,4,8,9,10,11,15,14,13,12},{16,17,18,19,23,22,21,20,24,25,..., dimensions={0} | all-to-all | bytes 524288 | tf_op jit(solution)/shard_map/all_to_all | solution.py:404
  75.6 0.6 gather.1
Async XLA Ops:
  1.5 12.6 %all-to-all-start = ((bf16[16,16,512]{2,1,0:T(8,128)(2,1)}), bf16[16,16,512]{2,1,0:T(8,128)(2,1)S(1)}, u32[]{:S(2)}, u32[]{:S(2)}) async-start(bf16[16,16,512]{2,1,0:T(8,128)(2,1)} %spread.1), calls=%async_computation | async-start | bytes 524288 | tf_op jit(solution)/shard_map/all_to_all | solution.py:324
  14.0 44.7 %copy-start = (bf16[256,8192]{1,0:T(8,128)(2,1)S(1)}, bf16[256,8192]{1,0:T(8,128)(2,1)}, u32[]{:S(2)}) copy-start(bf16[256,8192]{1,0:T(8,128)(2,1)} %w_ref.1) | copy-start | bytes 12582916
  57.5 1.3 %collective-permute-start = (bf16[256,128]{1,0:T(8,128)(2,1)S(1)}, bf16[256,128]{1,0:T(8,128)(2,1)S(1)}, u32[]{:S(2)}, u32[]{:S(2)}) collective-permute-start(bf16[256,128]{1,0:T(8,128)(2,1)S(1)} %bitcast.6), channel_id=1, source_target_pairs={{0,16},{16,0},{1,17},{17,1},{2,18},{18,2},{3,19},{19,3},{4,20},{20... | collective-permute-start | bytes 196616 | tf_op jit(solution)/shard_map/ppermute | solution.py:394

commit v7 on v6

--- a/solution.py
+++ b/solution.py
@@ -117,7 +117,9 @@
             next_slot = slot_ref[s, next_group]
             at_group = jnp.where(leaves, next_group, at_group)
             at_slot = jnp.where(leaves, next_slot, at_slot)
-            column = at_group * ROWS + s * REQ + at_slot
+            along = at_group >> 2
+            place = (along ^ (along >> 1)) * 4 + (at_group & 3)
+            column = place * ROWS + s * REQ + at_slot
             target = jnp.where((row8 & 3) == s, column, target)
         for part in range(GROUPS * ROWS // HD):
             pick_in_ref[r * 8 : r * 8 + 8, part * HD : (part + 1) * HD] = jnp.where(
@@ -321,7 +323,9 @@
         compiler_params=params(),
         name="spread",
     )(left(step_inputs))
-    x = lax.all_to_all(x, ("chip", "core"), 0, 0, tiled=True).reshape(GROUPS * ROWS, width)
+    order = [[4 * (k ^ (k >> 1)) + low for k in range(4) for low in range(4)]]
+    x = lax.all_to_all(x, ("chip", "core"), 0, 0, tiled=True, axis_index_groups=order)
+    x = x.reshape(GROUPS * ROWS, width)
 
     half = np.arange(HD) % (HD // 2)
     freq = jnp.asarray((rope_base ** (-2.0 * half / HD)).astype(np.float32).reshape(1, HD))

time: 76.7 us -> 76.6 us (level)
  waiting for transfers between devices: 5.41 us -> 4.64 us
    all_to_all x1, blocking collectives: 13 us -> 14.5 us  [body(): lax.all_to_all(attention.reshape(CHIPS * 4, 8, HD), ('chip', 'seq_z'), 0,...]
    all_to_all x1, blocking collectives: 27.8 us -> 26.8 us  [body(): received = lax.all_to_all(sent, seq, 0, 0, tiled=True)]
    all_to_all x1, waiting for transfers between devices: 4.16 us -> 3.39 us  [body(): lax.all_to_all(x, ('chip', 'core'), 0, 0, tiled=True, axis_index_groups=o...]
where the time goes in v7:
time: 76.6 us; the launch traced here: 76.1 us
  blocking collectives  57.5 us (75%)
  Pallas kernels  7.48 us (10%)
  starting transfers between devices  5.79 us (8%)
  waiting for transfers between devices  4.64 us (6%)
    all_to_all x1, blocking collectives, body(): received = lax.all_to_all(sent, seq, 0, 0, tiled=True)  26.8 us
    all_to_all x1, blocking collectives, body(): lax.all_to_all(shares, seq, 0, 0, tiled=True, axis_index_groups=[SEQ_ORDER])  16.2 us
    all_to_all x1, blocking collectives, body(): lax.all_to_all(attention.reshape(CHIPS * 4, 8, HD), ('chip', 'seq_z'), 0,...  14.5 us
    all_to_all x1, starting transfers between devices, body(): lax.all_to_all(x, ('chip', 'core'), 0, 0, tiled=True, axis_index_groups=o...  5.79 us
    all_to_all x1, waiting for transfers between devices, body(): lax.all_to_all(x, ('chip', 'core'), 0, 0, tiled=True, axis_index_groups=o...  3.39 us
    pallas_call x1, Pallas kernels, body(): pl.pallas_call(project_kernel, in_specs=[in_vmem()] * 6 + [anywhere()] *...  2.17 us
    pallas_call x1, Pallas kernels, body(): pl.pallas_call(prepare_kernel, in_specs=[anywhere()] * 3 + [pl.BlockSpec(...  1.94 us
  transfers between devices with their start and end apart: 2, of which 2 were waited for; matrix products, arithmetic and copies ran while one was open for 1% of the time, Pallas kernels for 3%

profile of v7, /device:TPU:32, one launch (start us, length us, event | category | flops | bytes accessed | tf_op | source)
XLA Modules:
  0.0 76.1 jit_solution(5917467014143286971)
XLA Ops:
  0.0 1.4 %spread.1 = bf16[16,16,512]{2,1,0:T(8,128)(2,1)} custom-call(bf16[4,4,512]{2,1,0:T(4,128)(2,1)} %x_hbm.1), custom_call_target="tpu_custom_call" | custom-call | tf_op jit(solution)/shard_map/spread/pallas_call | solution.py:317
  1.5 5.8 %all-to-all-start = ((bf16[16,16,512]{2,1,0:T(8,128)(2,1)}), bf16[16,16,512]{2,1,0:T(8,128)(2,1)S(1)}, u32[]{:S(2)}, u32[]{:S(2)}) async-start(bf16[16,16,512]{2,1,0:T(8,128)(2,1)} %spread.1), calls=%async_computation | async-start | bytes 524288 | tf_op jit(solution)/shard_map/all_to_all | solution.py:327
  7.2 0.7 reshape.21.gain_ref
  7.9 1.9 %prepare.1 = (f32[32,256]{1,0:T(8,128)S(1)}, bf16[32,512]{1,0:T(8,128)(2,1)S(1)}, f32[8,768]{1,0:T(8,128)S(1)}, bf16[512,1024]{1,0:T(8,128)(2,1)S(1)}, bf16[512,...) custom-call(s32[4,16]{1,0:T(4,128)} %slot_hbm.1, s32[4]{0:T(128)} %shift_hbm.1, s32[4]{0:T(128)} %len_hbm.1, ...), custom_call_target="tpu_custom_call" | custom-call | bytes 20000000 | tf_op jit(solution)/shard_map/prepare/pallas_call | solution.py:333
  9.9 3.4 %all-to-all-done = bf16[16,16,512]{2,1,0:T(8,128)(2,1)S(1)} async-done(((bf16[16,16,512]{2,1,0:T(8,128)(2,1)}), bf16[16,16,512]{2,1,0:T(8,128)(2,1)S(1)}, u32[]{:S(2)}, u32[]{:S(2)}) %all-to-all-start) | async-done | bytes 262176 | tf_op jit(solution)/shard_map/all_to_all | solution.py:327
  13.3 0.0 copy-start
  13.3 2.2 %project.1 = bf16[16,112,128]{2,1,0:T(8,128)(2,1)S(1)} custom-call(bf16[256,512]{1,0:T(8,128)(2,1)S(1)} %bitcast.5, f32[32,256]{1,0:T(8,128)S(1)} %get-tuple-element.13.pick_ref, bf16[1,512]{1,0:T(2,128)(2,1)S(1)} %reshape.21.gain_ref, bf16[512,1024]{1,0:T(8,128)(2,1)S(1)} %get-tuple-element.14.wkv_ref, bf16[512,1024]{1,0:T(8,128)(2,1)S(1)} %get-tuple-element.15.wq0_ref, ...), custom_call_target="tpu_custom_call" | custom-call | tf_op jit(solution)/shard_map/project/pallas_call | solution.py:366
  15.4 26.8 %all_to_all.20.in_ref = bf16[16,112,128]{2,1,0:T(8,128)(2,1)S(1)} all-to-all(bf16[16,112,128]{2,1,0:T(8,128)(2,1)S(1)} %project.1), channel_id=1, replica_groups=mesh['chip'=8,'core'=2,'seq_y'=4,'seq_z'=4] {'seq_y','seq_z'}, dimensions={0} | all-to-all | bytes 917504 | tf_op jit(solution)/shard_map/all_to_all | solution.py:385
  42.2 0.5 attend.1
  42.8 14.5 %all_to_all.21 = bf16[32,8,128]{2,1,0:T(8,128)(2,1)S(1)} all-to-all(bf16[32,8,128]{2,1,0:T(8,128)(2,1)S(1)} %bitcast.8), channel_id=1, replica_groups=mesh['chip'=8,'core'=2,'seq_y'=4,'seq_z'=4] {'chip','seq_z'}, dimensions={0} | all-to-all | bytes 131072 | tf_op jit(solution)/shard_map/all_to_all | solution.py:395
  57.3 0.0 collective-permute-start
  57.3 1.3 %collective-permute-done.other_ref = bf16[256,128]{1,0:T(8,128)(2,1)S(1)} collective-permute-done((bf16[256,128]{1,0:T(8,128)(2,1)S(1)}, bf16[256,128]{1,0:T(8,128)(2,1)S(1)}, u32[]{:S(2)}, u32[]{:S(2)}) %collective-permute-start) | collective-permute-done | bytes 65568 | tf_op jit(solution)/shard_map/ppermute | solution.py:398
  58.5 0.0 copy-done
  58.5 0.8 output.1
  59.3 16.2 %all_to_all.22.in_ref = bf16[16,16,512]{2,1,0:T(8,128)(2,1)S(1)} all-to-all(bf16[16,16,512]{2,1,0:T(8,128)(2,1)S(1)} %output.1), channel_id=1, replica_groups={{0,1,2,3,7,6,5,4,8,9,10,11,15,14,13,12},{16,17,18,19,23,22,21,20,24,25,..., dimensions={0} | all-to-all | bytes 524288 | tf_op jit(solution)/shard_map/all_to_all | solution.py:408
  75.5 0.6 gather.1
Async XLA Ops:
  1.5 11.8 %all-to-all-start = ((bf16[16,16,512]{2,1,0:T(8,128)(2,1)}), bf16[16,16,512]{2,1,0:T(8,128)(2,1)S(1)}, u32[]{:S(2)}, u32[]{:S(2)}) async-start(bf16[16,16,512]{2,1,0:T(8,128)(2,1)} %spread.1), calls=%async_computation | async-start | bytes 524288 | tf_op jit(solution)/shard_map/all_to_all | solution.py:327
  13.3 45.3 %copy-start = (bf16[256,8192]{1,0:T(8,128)(2,1)S(1)}, bf16[256,8192]{1,0:T(8,128)(2,1)}, u32[]{:S(2)}) copy-start(bf16[256,8192]{1,0:T(8,128)(2,1)} %w_ref.1) | copy-start | bytes 12582916
  57.3 1.3 %collective-permute-start = (bf16[256,128]{1,0:T(8,128)(2,1)S(1)}, bf16[256,128]{1,0:T(8,128)(2,1)S(1)}, u32[]{:S(2)}, u32[]{:S(2)}) collective-permute-start(bf16[256,128]{1,0:T(8,128)(2,1)S(1)} %bitcast.6), channel_id=1, source_target_pairs={{0,16},{16,0},{1,17},{17,1},{2,18},{18,2},{3,19},{19,3},{4,20},{20... | collective-permute-start | bytes 196616 | tf_op jit(solution)/shard_map/ppermute | solution.py:398
